TPU v7x, 128 devices: a whole 4x4x4 slice. The times are simulated.
128 devices in a mesh: tm: 4 (over z), space: 8 (over y, x_lo), clip: 4 (over x_hi, core).
Axes of the slice: x: 4 (x_hi: 2, x_lo: 2; x = x_hi * 2 + x_lo), y: 4, z: 4, core: 2. Of those that a mesh axis runs over, the one named last changes fastest.
Arguments:
- activations: bfloat16 [96, 256, 1408], P(('clip', 'tm'), 'space'), parts along dimension 0, may hold values from -200 to 200
- attn_gain: float32 [1408], replicated, may hold values from 0.5 to 2
- attn_shift: float32 [1408], replicated, may hold values from -3 to 3
- w_qkv: bfloat16 [1408, 4224], replicated, may hold values from -4 to 4
- b_qkv: float32 [4224], replicated, may hold values from -3 to 3
- w_out: bfloat16 [1408, 1408], replicated, may hold values from -2.5 to 2.5
- b_out: float32 [1408], replicated, may hold values from -3 to 3
- final_gain: float32 [1408], replicated, may hold values from 0.5 to 2
- final_shift: float32 [1408], replicated, may hold values from -3 to 3
- mask_tokens: int32 [128, 192], P('clip'), parts along dimension 0, may hold values from -1 to 6143, as said below
- assignment: int32 [128], P('clip'), parts along dimension 0, may hold values from 0 to 31, each once
Outputs:
- targets: bfloat16 [128, 192, 1408], P(('clip', 'tm', 'space')), parts along dimension 0
There are 4 independent parts, one for each index of `clip`. A program takes and returns all parts, laid end to end along the dimension named above; an argument that names none is the same for every part. Nothing has to cross between parts.
Inputs may be any that keep to these rules, and one draw needn't show every extreme that they name: `mask_tokens`: each row lists distinct tokens, no token in two rows; its listed entries come first in no fixed order, then -1 to the end. The block of tokens of one device (temporal positions k * 6 to k * 6 + 5 and patch positions m * 32 to m * 32 + 31) gives at most 6 entries to one row; in some row every such block gives exactly 6, so that row is full. `assignment`: each owner once.
All inputs are finite; a program needn't handle non-finite values.
Results may differ from a plain program's by a relative error of at most 0.0085.
The roundings to bfloat16 on the way count: a program that leaves them out, or rounds other values in their place, can miss the bound.
Values may be sent and summed in bfloat16 or wider, within the bound.
No kernel may reach another device: no remote copies, remote signals or barrier semaphores. Data moves between devices by JAX's collectives and lax.ppermute only.
A program may use at most 128 MiB of HBM per device.

v0:
```python
import math

import jax
import jax.numpy as jnp
from jax import lax
from jax.sharding import PartitionSpec as P

HEADS = 16


EPSILON = 1e-06
FLOOR_SCORE = -1e30


def items_in_groups(x, axis, split_dim, concat_dim, work, item_dim, out_dim):
    items = jax.tree.leaves(x)[0].shape[item_dim]
    count = 2 if items % 2 == 0 else 1
    done = []
    for k in range(count):
        group = jax.tree.map(
            lambda a: lax.slice_in_dim(
                a, k * (items // count), (k + 1) * (items // count), axis=item_dim
            ),
            x,
        )
        done.append(
            work(
                lax.all_to_all(
                    group, axis, split_axis=split_dim, concat_axis=concat_dim, tiled=True
                )
            )
        )
    return jax.tree.map(lambda *parts: jnp.concatenate(parts, axis=out_dim), *done)


def layer_norm(values, ln_gain, ln_shift):
    centre = jnp.mean(values, axis=-1, keepdims=True)
    deviation = values - centre
    variance = jnp.mean(deviation * deviation, axis=-1, keepdims=True)
    return deviation * lax.rsqrt(variance + EPSILON) * ln_gain + ln_shift


def start_state(query_heads):
    query_count, head_count, head_width = query_heads.shape
    return (
        jnp.full((head_count, query_count), FLOOR_SCORE, jnp.float32),
        jnp.zeros((head_count, query_count), jnp.float32),
        jnp.zeros((head_count, query_count, head_width), jnp.float32),
    )


def finish_state(carried_state):
    running_max, running_total, running_sum = carried_state
    return jnp.transpose(running_sum / running_total[:, :, None], (1, 0, 2)).astype(jnp.bfloat16)


def make_attend(query_heads):
    query_count, head_count, head_width = query_heads.shape
    score_scale = 1.0 / math.sqrt(head_width)

    def one_block(carried_state, kv_block):
        running_max, running_total, running_sum = carried_state
        block_length = kv_block.shape[1]
        key_rows = kv_block[0].reshape(block_length, head_count, head_width)
        value_rows = kv_block[1].reshape(block_length, head_count, head_width)
        scores = (
            jnp.einsum("qhe,khe->hqk", query_heads, key_rows, preferred_element_type=jnp.float32)
            * score_scale
        )
        new_max = jnp.maximum(running_max, jnp.max(scores, axis=-1))
        factor = jnp.exp(running_max - new_max)
        weights = jnp.exp(scores - new_max[:, :, None])
        running_total = running_total * factor + jnp.sum(weights, axis=-1)
        running_sum = running_sum * factor[:, :, None] + jnp.einsum(
            "hqk,khe->hqe",
            weights.astype(jnp.bfloat16),
            value_rows,
            preferred_element_type=jnp.float32,
        )
        return (new_max, running_total, running_sum)

    def attend(carried_state, key_piece, first_row):
        length = key_piece.shape[1]
        block_rows = length
        while block_rows > 1024 and block_rows % 2 == 0:
            block_rows = block_rows // 2

        def advance(position, carried):
            kv_block = lax.dynamic_slice_in_dim(key_piece, position * block_rows, block_rows, 1)
            return one_block(carried, kv_block)

        return lax.fori_loop(0, length // block_rows, advance, carried_state)

    return attend


def local(
    activations,
    attn_gain,
    attn_shift,
    w_qkv,
    b_qkv,
    w_out,
    b_out,
    final_gain,
    final_shift,
    mask_tokens,
    assignment,
):
    frame_count, patch_count, model_width = activations.shape
    local_rows = frame_count * patch_count
    head_width = model_width // HEADS
    tokens_flat = activations.reshape(local_rows, model_width)
    normed_in = layer_norm(tokens_flat.astype(jnp.float32), attn_gain, attn_shift).astype(
        jnp.bfloat16
    )
    projected = (jnp.dot(normed_in, w_qkv, preferred_element_type=jnp.float32) + b_qkv).astype(
        jnp.bfloat16
    )
    query_rows = projected[:, :model_width]
    paired = jnp.stack(
        (projected[:, model_width : 2 * model_width], projected[:, 2 * model_width :])
    )
    groups = lax.axis_size("space")
    group_heads = HEADS // groups
    stacked = jnp.stack((query_rows, paired[0], paired[1])).reshape(
        3, local_rows, groups, group_heads, head_width
    )

    def head_work(swapped):
        gathered_rows = swapped.shape[1]
        kept_heads = swapped.shape[3]
        query_heads = swapped[0].reshape(gathered_rows, kept_heads, head_width)
        kv_rows = swapped[1:].reshape(2, gathered_rows, kept_heads * head_width)
        time_state = make_attend(query_heads)(
            start_state(query_heads),
            lax.all_gather(kv_rows, "tm", axis=1, tiled=True),
            jnp.int32(0),
        )
        head_output = finish_state(time_state).reshape(gathered_rows, 1, kept_heads, head_width)
        return lax.all_to_all(head_output, "space", split_axis=0, concat_axis=1, tiled=True)

    merged = items_in_groups(stacked, "space", 2, 1, head_work, 3, 2)
    attended = merged.reshape(local_rows, model_width)
    hidden = (
        tokens_flat.astype(jnp.float32)
        + jnp.dot(attended, w_out, preferred_element_type=jnp.float32)
        + b_out
    ).astype(jnp.bfloat16)
    normed = layer_norm(hidden.astype(jnp.float32), final_gain, final_shift).astype(jnp.bfloat16)
    owners = mask_tokens.shape[0]
    capacity = mask_tokens.shape[1]
    per_source = capacity // owners
    spaces = lax.axis_size("space")
    spatial = patch_count * spaces
    own_index = lax.axis_index("tm") * spaces + lax.axis_index("space")
    owner_lists = jnp.take(mask_tokens, assignment, axis=0)
    listed = owner_lists >= 0
    clipped = jnp.maximum(owner_lists, 0)
    token_frame = clipped // spatial
    token_patch = clipped % spatial
    home_device = token_frame // frame_count * spaces + token_patch // patch_count
    local_row = token_frame % frame_count * patch_count + token_patch % patch_count
    mine = listed & (home_device == own_index)
    slot_index = jnp.cumsum(mine.astype(jnp.int32), axis=1) - 1
    wanted = mine[:, None, :] & (
        slot_index[:, None, :] == jnp.arange(per_source, dtype=jnp.int32)[None, :, None]
    )
    picks = jnp.sum(jnp.where(wanted, local_row[:, None, :], 0), axis=-1)
    present = jnp.any(wanted, axis=-1)
    own_home = lax.dynamic_index_in_dim(home_device, own_index, 0, keepdims=False)
    own_listed = lax.dynamic_index_in_dim(listed, own_index, 0, keepdims=False)
    entry_order = jnp.arange(capacity, dtype=jnp.int32)
    earlier = (
        (entry_order[:, None] < entry_order[None, :])
        & own_listed[:, None]
        & (own_home[:, None] == own_home[None, :])
    )
    entry_rank = jnp.sum(earlier.astype(jnp.int32), axis=0)
    where_from = jnp.where(own_listed, own_home * per_source + entry_rank, 0)
    outgoing = jnp.where(
        present[:, :, None], jnp.take(normed, picks, axis=0), jnp.zeros((), jnp.bfloat16)
    )
    arrived = lax.all_to_all(outgoing, ("tm", "space"), split_axis=0, concat_axis=0, tiled=True)
    row_table = arrived.reshape(owners * per_source, model_width)
    placed = jnp.take(row_table, where_from, axis=0)
    return jnp.where(own_listed[:, None], placed, jnp.zeros((), jnp.bfloat16))[None]


def solution(mesh):
    in_specs = (
        P(("clip", "tm"), "space", None),
        P(),
        P(),
        P(),
        P(),
        P(),
        P(),
        P(),
        P(),
        P("clip", None),
        P("clip"),
    )
    out_specs = P(("clip", "tm", "space"), None, None)
    return jax.shard_map(local, mesh=mesh, in_specs=in_specs, out_specs=out_specs, check_vma=False)
```

profile of v0, /device:TPU:0, one launch (start us, length us, event | category | flops | bytes accessed | tf_op | source)
XLA Modules:
  0.0 275.3 jit_solution(16591129981595023906)
XLA Ops:
  10.7 7.2 %fusion.28 = bf16[192,4224]{1,0:T(8,128)(2,1)S(1)} fusion(bf16[192,1408]{1,0:T(8,128)(2,1)S(1)} %fusion.35, bf16[1408,4224]{1,0:T(8,128)(2,1)} %param.18, f32[4224]{0:T(1024)} %param.19), kind=kOutput, calls=%fused_computation.50 | convolution fusion | flops 2285420544 | bytes 14074368 | tf_op jit(solution)/shard_map/dot_general | solution.py:117
  21.1 4.5 %stack.13 = bf16[1,192,8,2,88]{4,3,2,1,0:T(2,128)(2,1)S(1)} reshape(bf16[192,1408]{1,0:T(8,128)(2,1)} %get-tuple-element.371) | data formatting | bytes 1081344 | tf_op jit(solution)/shard_map/stack | solution.py:126
  25.6 5.0 %stack.14 = bf16[1,192,8,2,88]{4,3,2,1,0:T(2,128)(2,1)} reshape(bf16[192,1408]{1,0:T(8,128)(2,1)} %get-tuple-element.370) | data formatting | bytes 1081344 | tf_op jit(solution)/shard_map/stack | solution.py:126
  32.9 5.4 %fusion.52 = (bf16[3,192,8,1,88]{4,3,2,1,0:T(2,128)(2,1)}, bf16[3,192,8,1,88]{4,3,2,1,0:T(2,128)(2,1)}) fusion(bf16[3,192,8,2,88]{4,3,2,1,0:T(2,128)(2,1)S(1)} %constant_dynamic-update-slice_fusion), kind=kLoop, calls=%fused_computation.136 | loop fusion | bytes 3244032 | tf_op jit(solution)/shard_map/slice | solution.py:21
  38.3 4.7 %copy.99 = bf16[3,192,8,1,88]{1,4,3,0,2:T(8,128)(2,1)S(1)} copy(bf16[3,192,8,1,88]{4,3,2,1,0:T(2,128)(2,1)} %get-tuple-element.369) | data formatting | bytes 1622016 | tf_op jit(solution)/shard_map/slice | solution.py:21
  43.0 21.5 %all_to_all.71 = bf16[3,192,8,1,88]{1,4,3,0,2:T(8,128)(2,1)S(1)} all-to-all(bf16[3,192,8,1,88]{1,4,3,0,2:T(8,128)(2,1)S(1)} %copy.99), channel_id=1, replica_groups=mesh['tm'=4,'space'=8,'clip'=4] {'space'}, dimensions={2} | all-to-all | bytes 1622016 | tf_op jit(solution)/shard_map/all_to_all | solution.py:28
  68.1 4.4 %copy.91 = bf16[3,192,8,1,88]{1,4,3,0,2:T(8,128)(2,1)} copy(bf16[3,192,8,1,88]{4,3,2,1,0:T(2,128)(2,1)S(1)} %copy-done.4) | data formatting | bytes 1622016 | tf_op jit(solution)/shard_map/slice | solution.py:21
  72.5 4.2 %all-to-all-start = ((bf16[3,192,8,1,88]{1,4,3,0,2:T(8,128)(2,1)}), bf16[3,192,8,1,88]{1,4,3,0,2:T(8,128)(2,1)}, u32[]{:S(2)}, u32[]{:S(2)}) async-start(bf16[3,192,8,1,88]{1,4,3,0,2:T(8,128)(2,1)} %copy.91), calls=%async_computation | async-start | bytes 2162688 | tf_op jit(solution)/shard_map/all_to_all | solution.py:28
  80.8 10.9 %all-to-all-done = bf16[3,192,8,1,88]{1,4,3,0,2:T(8,128)(2,1)} async-done(((bf16[3,192,8,1,88]{1,4,3,0,2:T(8,128)(2,1)}), bf16[3,192,8,1,88]{1,4,3,0,2:T(8,128)(2,1)}, u32[]{:S(2)}, u32[]{:S(2)}) %all-to-all-start) | async-done | bytes 811040 | tf_op jit(solution)/shard_map/all_to_all | solution.py:28
  95.5 4.6 %all-gather.5.cloned.1.call-done = bf16[2,6144,88]{1,2,0:T(8,128)(2,1)} async-done(((bf16[2,1536,88]{1,2,0:T(8,128)(2,1)}), bf16[2,6144,88]{1,2,0:T(8,128)(2,1)}) %all-gather.5.cloned.1.call-update) | async-done | bytes 2162704 | tf_op jit(solution)/shard_map/all_gather | solution.py:137
  100.1 58.3 %while.37 = (s32[]{:T(128)}, f32[1,1536]{1,0:T(1,128)S(1)}, f32[1,1536]{1,0:T(1,128)S(1)}, f32[1,1536,88]{1,2,0:T(8,128)S(1)}, bf16[2,6144,88]{1,2,0:T(8,128)(2,...) while((s32[]{:T(128)}, f32[1,1536]{1,0:T(1,128)S(1)}, ...), condition=%wide.region_14.15_spmd.clone, body=%wide.region_11.14_spmd.clone.sunk | while | flops 425088000 | bytes 34756832 | solution.py:92
  104.0 3.3 %fusion.78 = f32[1,1536,88]{1,2,0:T(8,128)S(1)} fusion(f32[768,1536]{1,0:T(8,128)} %copy-done.2, f32[1536]{0:T(1024)S(1)} %get-tuple-element.471, f32[1,1536,88]{1,2,0:T(8,128)S(1)} %get-tuple-element.487, f32[1536]{0:T(1024)S(1)} %get-tuple-element.472, pred[]{:T(512)S(6)} %compare.27, bf16[2,6144,88]{1,2,0:T(8,128)(2,1)} %get-tuple-element.499, ...), kind=kOutput, calls=%fused_computation.31.clone.1 | convolution fusion | flops 211562496 | bytes 5947401 | tf_op jit(solution)/shard_map/while/body/eval_jaxpr/hqk,khe->hqe/dot_general | solution.py:74
  111.2 3.5 %fusion.78 = f32[1,1536,88]{1,2,0:T(8,128)S(1)} fusion(f32[768,1536]{1,0:T(8,128)} %copy-done.2, f32[1536]{0:T(1024)S(1)} %get-tuple-element.471, f32[1,1536,88]{1,2,0:T(8,128)S(1)} %get-tuple-element.487, f32[1536]{0:T(1024)S(1)} %get-tuple-element.472, pred[]{:T(512)S(6)} %compare.27, bf16[2,6144,88]{1,2,0:T(8,128)(2,1)} %get-tuple-element.499, ...), kind=kOutput, calls=%fused_computation.31.clone.1 | convolution fusion | flops 211562496 | bytes 5947401 | tf_op jit(solution)/shard_map/while/body/eval_jaxpr/hqk,khe->hqe/dot_general | solution.py:74
  118.7 3.4 %fusion.78 = f32[1,1536,88]{1,2,0:T(8,128)S(1)} fusion(f32[768,1536]{1,0:T(8,128)} %copy-done.2, f32[1536]{0:T(1024)S(1)} %get-tuple-element.471, f32[1,1536,88]{1,2,0:T(8,128)S(1)} %get-tuple-element.487, f32[1536]{0:T(1024)S(1)} %get-tuple-element.472, pred[]{:T(512)S(6)} %compare.27, bf16[2,6144,88]{1,2,0:T(8,128)(2,1)} %get-tuple-element.499, ...), kind=kOutput, calls=%fused_computation.31.clone.1 | convolution fusion | flops 211562496 | bytes 5947401 | tf_op jit(solution)/shard_map/while/body/eval_jaxpr/hqk,khe->hqe/dot_general | solution.py:74
  126.0 3.4 %fusion.78 = f32[1,1536,88]{1,2,0:T(8,128)S(1)} fusion(f32[768,1536]{1,0:T(8,128)} %copy-done.2, f32[1536]{0:T(1024)S(1)} %get-tuple-element.471, f32[1,1536,88]{1,2,0:T(8,128)S(1)} %get-tuple-element.487, f32[1536]{0:T(1024)S(1)} %get-tuple-element.472, pred[]{:T(512)S(6)} %compare.27, bf16[2,6144,88]{1,2,0:T(8,128)(2,1)} %get-tuple-element.499, ...), kind=kOutput, calls=%fused_computation.31.clone.1 | convolution fusion | flops 211562496 | bytes 5947401 | tf_op jit(solution)/shard_map/while/body/eval_jaxpr/hqk,khe->hqe/dot_general | solution.py:74
  161.4 5.2 %all-to-all-start.3 = ((bf16[8,2,8448]{2,1,0:T(2,128)(2,1)}), bf16[8,2,8448]{2,1,0:T(2,128)(2,1)S(1)}, u32[]{:S(2)}, u32[]{:S(2)}) async-start(bf16[8,2,8448]{2,1,0:T(2,128)(2,1)} %reshape.470), calls=%async_computation.3 | async-start | bytes 540672 | tf_op jit(solution)/shard_map/all_to_all | solution.py:141
  166.6 58.0 %while.36 = (s32[]{:T(128)}, f32[1,1536]{1,0:T(1,128)S(1)}, f32[1,1536]{1,0:T(1,128)S(1)}, f32[1,1536,88]{1,2,0:T(8,128)S(1)}, bf16[2,6144,88]{1,2,0:T(8,128)(2,...) while((s32[]{:T(128)}, f32[1,1536]{1,0:T(1,128)S(1)}, ...), condition=%wide.region_10.0_spmd.clone, body=%wide.region_7.10_spmd.clone.sunk | while | flops 425088000 | bytes 34756832 | solution.py:92
  177.8 3.3 %fusion.73 = f32[1,1536,88]{1,2,0:T(8,128)S(1)} fusion(f32[768,1536]{1,0:T(8,128)} %copy-done.3, f32[1536]{0:T(1024)S(1)} %get-tuple-element.460, f32[1,1536,88]{1,2,0:T(8,128)S(1)} %get-tuple-element.520, f32[1536]{0:T(1024)S(1)} %get-tuple-element.461, pred[]{:T(512)S(6)} %compare.26, bf16[2,6144,88]{1,2,0:T(8,128)(2,1)} %get-tuple-element.532, ...), kind=kOutput, calls=%fused_computation.8.clone.1 | convolution fusion | flops 211562496 | bytes 5947401 | tf_op jit(solution)/shard_map/while/body/eval_jaxpr/hqk,khe->hqe/dot_general | solution.py:74
  199.5 3.3 %fusion.73 = f32[1,1536,88]{1,2,0:T(8,128)S(1)} fusion(f32[768,1536]{1,0:T(8,128)} %copy-done.3, f32[1536]{0:T(1024)S(1)} %get-tuple-element.460, f32[1,1536,88]{1,2,0:T(8,128)S(1)} %get-tuple-element.520, f32[1536]{0:T(1024)S(1)} %get-tuple-element.461, pred[]{:T(512)S(6)} %compare.26, bf16[2,6144,88]{1,2,0:T(8,128)(2,1)} %get-tuple-element.532, ...), kind=kOutput, calls=%fused_computation.8.clone.1 | convolution fusion | flops 211562496 | bytes 5947401 | tf_op jit(solution)/shard_map/while/body/eval_jaxpr/hqk,khe->hqe/dot_general | solution.py:74
  227.2 5.7 %all-to-all-start.1 = ((bf16[8,2,8448]{2,1,0:T(2,128)(2,1)}), bf16[8,2,8448]{2,1,0:T(2,128)(2,1)S(1)}, u32[]{:S(2)}, u32[]{:S(2)}) async-start(bf16[8,2,8448]{2,1,0:T(2,128)(2,1)} %reshape.472), calls=%async_computation.1 | async-start | bytes 540672 | tf_op jit(solution)/shard_map/all_to_all | solution.py:141
  235.8 4.4 %all-to-all-done.1 = bf16[8,2,8448]{2,1,0:T(2,128)(2,1)S(1)} async-done(((bf16[8,2,8448]{2,1,0:T(2,128)(2,1)}), bf16[8,2,8448]{2,1,0:T(2,128)(2,1)S(1)}, u32[]{:S(2)}, u32[]{:S(2)}) %all-to-all-start.1) | async-done | bytes 270368 | tf_op jit(solution)/shard_map/all_to_all | solution.py:141
  242.8 3.4 %fusion.54 = (f32[192]{0:T(256)S(1)}, f32[192,1408]{1,0:T(8,128)S(1)}) fusion(f32[1408]{0:T(1024)S(1)} %copy-done.7, bf16[192,1408]{0,1:T(8,128)(2,1)S(1)} %bitcast.148, bf16[1408,1408]{1,0:T(8,128)(2,1)} %param.20, bf16[192,1408]{1,0:T(8,128)(2,1)S(1)} %bitcast.143), kind=kOutput, calls=%fused_computation.138 | convolution fusion | flops 762888000 | bytes 6134016 | tf_op jit(solution)/shard_map/dot_general | solution.py:147
  249.1 4.4 %all-to-all-start.4 = ((bf16[32,6,1408]{2,1,0:T(8,128)(2,1)}), bf16[32,6,1408]{2,1,0:T(8,128)(2,1)S(1)}, u32[]{:S(2)}, u32[]{:S(2)}) async-start(bf16[32,6,1408]{2,1,0:T(8,128)(2,1)} %select_select_fusion), calls=%async_computation.4 | async-start | bytes 1441792 | tf_op jit(solution)/shard_map/all_to_all | solution.py:184
  253.6 12.6 %all-to-all-done.4 = bf16[32,6,1408]{2,1,0:T(8,128)(2,1)S(1)} async-done(((bf16[32,6,1408]{2,1,0:T(8,128)(2,1)}), bf16[32,6,1408]{2,1,0:T(8,128)(2,1)S(1)}, u32[]{:S(2)}, u32[]{:S(2)}) %all-to-all-start.4) | async-done | bytes 540704 | tf_op jit(solution)/shard_map/all_to_all | solution.py:184
  (236 shorter events, 132.0 us)
Async XLA Ops:
  6.5 70.3 %copy-start = (s32[32,192]{1,0:T(8,128)S(1)}, s32[32,192]{1,0:T(8,128)}, u32[]{:S(2)}) copy-start(s32[32,192]{1,0:T(8,128)} %param.24) | copy-start | bytes 73732
  6.5 93.6 %all-gather.5.cloned.1.call-start = ((), (), s32[]{:S(2)}) async-start(), calls=%async_computation.6 | async-start | bytes 2703360 | tf_op jit(solution)/shard_map/all_gather | solution.py:137
  64.6 3.5 %copy-start.4 = (bf16[3,192,8,1,88]{4,3,2,1,0:T(2,128)(2,1)S(1)}, bf16[3,192,8,1,88]{4,3,2,1,0:T(2,128)(2,1)}, u32[]{:S(2)}) copy-start(bf16[3,192,8,1,88]{4,3,2,1,0:T(2,128)(2,1)} %get-tuple-element.368) | copy-start | bytes 2433028
  68.1 8.7 %copy-start.11 = (s32[32]{0:T(128)S(1)}, s32[32]{0:T(128)}, u32[]{:S(2)}) copy-start(s32[32]{0:T(128)} %param.25) | copy-start | bytes 388
  72.5 19.2 %all-to-all-start = ((bf16[3,192,8,1,88]{1,4,3,0,2:T(8,128)(2,1)}), bf16[3,192,8,1,88]{1,4,3,0,2:T(8,128)(2,1)}, u32[]{:S(2)}, u32[]{:S(2)}) async-start(bf16[3,192,8,1,88]{1,4,3,0,2:T(8,128)(2,1)} %copy.91), calls=%async_computation | async-start | bytes 2162688 | tf_op jit(solution)/shard_map/all_to_all | solution.py:28
  76.8 89.8 %all-gather.3.cloned.1.call-start = ((), (), s32[]{:S(2)}) async-start(), calls=%async_computation.5 | async-start | bytes 2703360 | tf_op jit(solution)/shard_map/all_gather | solution.py:137
  80.8 12.4 %copy-start.6 = (bf16[1,8,192,1,1,88]{2,5,4,3,1,0:T(8,128)(2,1)S(1)}, bf16[1,8,192,1,1,88]{2,5,4,3,1,0:T(8,128)(2,1)}, u32[]{:S(2)}) copy-start(bf16[1,8,192,1,1,88]{2,5,4,3,1,0:T(8,128)(2,1)} %slice.100) | copy-start | bytes 811012
  101.8 2.1 copy-start.2
  116.5 2.1 copy-start.2
  123.8 2.1 copy-start.2
  138.4 2.1 copy-start.2
  145.6 2.1 copy-start.2
  152.9 2.1 copy-start.2
  161.4 65.7 %all-to-all-start.3 = ((bf16[8,2,8448]{2,1,0:T(2,128)(2,1)}), bf16[8,2,8448]{2,1,0:T(2,128)(2,1)S(1)}, u32[]{:S(2)}, u32[]{:S(2)}) async-start(bf16[8,2,8448]{2,1,0:T(2,128)(2,1)} %reshape.470), calls=%async_computation.3 | async-start | bytes 540672 | tf_op jit(solution)/shard_map/all_to_all | solution.py:141
  168.4 2.1 copy-start.3
  175.6 2.1 copy-start.3
  182.9 2.1 copy-start.3
  190.1 2.1 copy-start.3
  224.6 8.5 %copy-start.10 = (pred[32,6]{0,1:T(8,128)(4,1)S(1)}, pred[32,6]{0,1:T(8,128)(4,1)}, u32[]{:S(2)}) copy-start(pred[32,6]{0,1:T(8,128)(4,1)} %fusion.42) | copy-start | bytes 580
  227.2 13.0 %all-to-all-start.1 = ((bf16[8,2,8448]{2,1,0:T(2,128)(2,1)}), bf16[8,2,8448]{2,1,0:T(2,128)(2,1)S(1)}, u32[]{:S(2)}, u32[]{:S(2)}) async-start(bf16[8,2,8448]{2,1,0:T(2,128)(2,1)} %reshape.472), calls=%async_computation.1 | async-start | bytes 540672 | tf_op jit(solution)/shard_map/all_to_all | solution.py:141
  242.8 3.7 %copy-start.8 = (f32[1408]{0:T(1024)S(1)}, f32[1408]{0:T(1024)}, u32[]{:S(2)}) copy-start(f32[1408]{0:T(1024)} %param.23) | copy-start | bytes 16900
  242.8 3.7 %copy-start.9 = (f32[1408]{0:T(1024)S(1)}, f32[1408]{0:T(1024)}, u32[]{:S(2)}) copy-start(f32[1408]{0:T(1024)} %param.22) | copy-start | bytes 16900
  249.1 17.0 %all-to-all-start.4 = ((bf16[32,6,1408]{2,1,0:T(8,128)(2,1)}), bf16[32,6,1408]{2,1,0:T(8,128)(2,1)S(1)}, u32[]{:S(2)}, u32[]{:S(2)}) async-start(bf16[32,6,1408]{2,1,0:T(8,128)(2,1)} %select_select_fusion), calls=%async_computation.4 | async-start | bytes 1441792 | tf_op jit(solution)/shard_map/all_to_all | solution.py:184
  266.2 2.3 copy-start.1
  (8 other events, 14.9 us)
Sparse Core Ops, SparseCore 0:
  68.2 31.8 all-gather.4
  101.8 31.4 all-gather.2
where the time goes:
time: 276 us; the launch traced here: 275 us
  matrix products  91.7 us (33%)
  local copies, waits for them, and re-layouts  70.4 us (26%)
  waiting for transfers between devices  32.5 us (12%)
  other arithmetic  24.7 us (9%)
  blocking collectives  21.5 us (8%)
  starting transfers between devices  19.5 us (7%)
  between operations  14 us (5%)
    dot_general x16, matrix products, one_block(): jnp.einsum('hqk,khe->hqe', weights.astype(jnp.bfloat16), value_rows, pref...  53.7 us
    dot_general x16, matrix products, one_block(): jnp.einsum('qhe,khe->hqk', query_heads, key_rows, preferred_element_type=...  27.5 us
    all_to_all x1, blocking collectives, items_in_groups(): lax.all_to_all(group, axis, split_axis=split_dim, concat_axis=concat_dim,...  21.5 us
    while x48, local copies, waits for them, and re-layouts  20.2 us
    slice x3, local copies, waits for them, and re-layouts, items_in_groups(): lax.slice_in_dim(a, k * (items // count), (k + 1) * (items // count), axi...  14.5 us
    reduce_sum x16, other arithmetic, one_block(): running_total = running_total * factor + jnp.sum(weights, axis=-1)  12.9 us
    another operation x4, local copies, waits for them, and re-layouts, local(): jnp.stack((query_rows, paired[0], paired[1]))  12.7 us
    all_to_all x1, waiting for transfers between devices, local(): lax.all_to_all(outgoing, ('tm', 'space'), split_axis=0, concat_axis=0, ti...  12.6 us
  transfers between devices with their start and end apart: 6, of which 4 were waited for; matrix products, arithmetic and copies ran while one was open for 42% of the time, Pallas kernels for 0%

commit v1 on v0

v1 whole, which is shorter than its diff:
```python
import functools
import math

import jax
import jax.numpy as jnp
from jax import lax
from jax.experimental import pallas as pl
from jax.experimental.pallas import tpu as pltpu
from jax.sharding import Mesh
from jax.sharding import PartitionSpec as P

EPSILON = 1e-06
D = 1408
HEADS = 16
HD = 88
HP = 96
TOK = 192
MAIN = 128
SRC = 16
HALF = SRC * TOK
BQ = 1024
OWNERS = 32
CAP = 192
SLOTS = 24
GROUPS = 4
QK_SCALE = math.log2(math.e) / math.sqrt(HD)
SAFE = 90.0
MIB = 1 << 20

f32 = jnp.float32
bf16 = jnp.bfloat16


def params(vmem_mib):
    return pltpu.CompilerParams(vmem_limit_bytes=vmem_mib * MIB)


def vmem():
    return pl.BlockSpec(memory_space=pltpu.VMEM)


def layer_norm(values, ln_gain, ln_shift):
    centre = jnp.mean(values, axis=-1, keepdims=True)
    deviation = values - centre
    variance = jnp.mean(deviation * deviation, axis=-1, keepdims=True)
    return deviation * lax.rsqrt(variance + EPSILON) * ln_gain + ln_shift


def lanes_below(shape, bound):
    return lax.broadcasted_iota(jnp.int32, shape, 1) < bound


def column_chunks(first, count):
    done = 0
    while done < count:
        width = min(256, count - done)
        yield first + done, done, width
        done += width


def start_weights(w_ref, buffer, sems, first, count):
    copies = []
    for i, (source, target, width) in enumerate(column_chunks(first, count)):
        copy = pltpu.make_async_copy(
            w_ref.at[:, pl.ds(source, width)], buffer.at[:, pl.ds(target, width)], sems.at[i]
        )
        copy.start()
        copies.append(copy)
    return copies


def project(copies, normed, buffer, bias_ref, first, count, main, rest):
    for copy, (source, target, width) in zip(copies, column_chunks(first, count)):
        copy.wait()
        part = jnp.dot(
            normed, buffer[:, target : target + width], preferred_element_type=f32
        ) + bias_ref[:, source : source + width]
        part = part.astype(bf16).astype(f32)
        tail = part[MAIN:]
        main[target : target + width, :] = part[:MAIN].T
        rest[target : target + width, :] = jnp.concatenate((tail, tail), axis=0).T


def kv_kernel(x_ref, gain_ref, shift_ref, w_ref, bias_ref, kv_ref, normed_ref, buffer, main, rest, sems):
    copies = start_weights(w_ref, buffer, sems, D, 2 * D)
    normed = layer_norm(x_ref[...].astype(f32), gain_ref[...], shift_ref[...]).astype(bf16)
    normed_ref[...] = normed
    project(copies, normed, buffer, bias_ref, D, 2 * D, main, rest)
    ones = jnp.ones((HP - HD, 128), f32)
    low = lanes_below((HP, 128), 64)
    for h in range(HEADS):
        k_rows, v_rows = slice(h * HD, h * HD + HD), slice(D + h * HD, D + h * HD + HD)
        kv_ref[h, 0:HP, :] = jnp.concatenate((main[k_rows, :], ones), axis=0).astype(bf16)
        kv_ref[h, HP : 2 * HP, :] = jnp.concatenate((main[v_rows, :], ones), axis=0).astype(bf16)
        kv_ref[h, 2 * HP : 3 * HP, :] = jnp.where(
            low,
            jnp.concatenate((rest[k_rows, :], ones), axis=0),
            jnp.concatenate((rest[v_rows, :], ones), axis=0),
        ).astype(bf16)


def q_kernel(normed_ref, w_ref, bias_ref, q_ref, buffer, main, rest, sems):
    copies = start_weights(w_ref, buffer, sems, 0, D)
    project(copies, normed_ref[...], buffer, bias_ref, 0, D, main, rest)
    zeros = jnp.zeros((HP - HD, 128), f32)
    low = lanes_below((HP // 2, 128), 64)
    for h in range(HEADS):
        rows = slice(h * HD, h * HD + HD)
        q_ref[h, 0:HP, :] = jnp.concatenate((main[rows, :], zeros), axis=0).astype(bf16)
        tail = jnp.concatenate((rest[rows, :], zeros), axis=0)
        q_ref[h, HP : HP + HP // 2, :] = jnp.where(low, tail[: HP // 2], tail[HP // 2 :]).astype(bf16)


def unpack_pair(first, second):
    low = lanes_below(first.shape, 64)
    return (
        jnp.where(low, first, pltpu.roll(second, 64, 1)),
        jnp.where(low, pltpu.roll(first, 64, 1), second),
    )


def unpack_kv(kv_ref, keys, values):
    def put(tile, k_tile, v_tile):
        at = pl.ds(pl.multiple_of(tile * 128, 128), 128)
        turned = jnp.concatenate((k_tile, jnp.zeros((128 - HP, 128), f32)), axis=0).T.astype(bf16)
        keys[at, 0:128] = turned
        keys[at, 128:256] = turned
        values[:, at] = v_tile
        return jnp.sum(k_tile[:HD] * k_tile[:HD], axis=0, keepdims=True)

    def pair(p, largest):
        for j in (2 * p, 2 * p + 1):
            square = put(j, kv_ref[j, 0:HP, :].astype(f32), kv_ref[j, HP : 2 * HP, :])
            largest = jnp.maximum(largest, square)
        k_tile, v_tile = unpack_pair(
            kv_ref[2 * p, 2 * HP :, :].astype(f32), kv_ref[2 * p + 1, 2 * HP :, :].astype(f32)
        )
        return jnp.maximum(largest, put(SRC + p, k_tile, v_tile.astype(bf16)))

    largest = lax.fori_loop(0, SRC // 2, pair, jnp.zeros((1, 128), f32))
    return jnp.max(largest, axis=1, keepdims=True)


def unpack_q(q_ref, queries):
    def put(tile, q_tile):
        at = pl.ds(pl.multiple_of(tile * 128, 128), 128)
        scaled = q_tile * QK_SCALE
        high = scaled.astype(bf16)
        zeros = jnp.zeros((128 - HP, 128), bf16)
        queries[0:HP, at] = high
        queries[HP:128, at] = zeros
        queries[128 : 128 + HP, at] = (scaled - high.astype(f32)).astype(bf16)
        queries[128 + HP : 256, at] = zeros

    def pair(p, carried):
        put(2 * p, q_ref[2 * p, 0:HP, :].astype(f32))
        put(2 * p + 1, q_ref[2 * p + 1, 0:HP, :].astype(f32))
        top, bottom = unpack_pair(
            q_ref[2 * p, HP:, :].astype(f32), q_ref[2 * p + 1, HP:, :].astype(f32)
        )
        put(SRC + p, jnp.concatenate((top, bottom), axis=0))
        return carried

    lax.fori_loop(0, SRC // 2, pair, 0)


def set_shift(queries, at, shift):
    high = shift.astype(bf16).astype(f32)
    middle = (shift - high).astype(bf16).astype(f32)
    low = shift - high - middle
    row = lax.broadcasted_iota(jnp.int32, (8, shift.shape[1]), 0)
    rows = jnp.where(row == 0, -high, jnp.where(row == 1, -middle, jnp.where(row == 2, -low, 0.0)))
    old = queries[HP - 16 : HP, at].astype(f32)
    queries[HP - 16 : HP, at] = jnp.concatenate((old[:8], rows), axis=0).astype(bf16)


def scores_of(keys, queries, first, count, at):
    return jnp.dot(keys[pl.ds(first, count), :], queries[:, at], preferred_element_type=f32)


def keep_safe(keys, queries, at, shift_ref, acc_ref, largest_key):
    block = queries[:, at].astype(f32)
    row = lax.broadcasted_iota(jnp.int32, (128, BQ), 0)
    whole = jnp.where(row < HD, block[0:128] + block[128:256], 0.0)
    norm = jnp.sqrt(jnp.sum(whole * whole, axis=0, keepdims=True) * largest_key)
    over = jnp.max(norm * 1.01 - shift_ref[:, at])

    @pl.when(jnp.logical_not(over <= SAFE))
    def _():
        def step(i, above):
            got = scores_of(keys, queries, pl.multiple_of(i * 256, 256), 256, at)
            return jnp.maximum(above, jnp.max(got, axis=0, keepdims=True))

        above = lax.fori_loop(0, HALF // 256, step, jnp.zeros((1, BQ), f32))
        moved = shift_ref[:, at] + above
        if acc_ref is not None:
            acc_ref[:, at] = acc_ref[:, at] * jnp.exp2(-above)
        shift_ref[:, at] = moved
        set_shift(queries, at, moved)


def weighted(keys, queries, values, at):
    weights = jnp.exp2(scores_of(keys, queries, 0, HALF, at)).astype(bf16)
    return jnp.dot(values[...], weights, preferred_element_type=f32)


def own_kernel(q_ref, kv_ref, queries_ref, shift_ref, acc_ref, keys, values):
    largest_key = unpack_kv(kv_ref, keys, values)
    unpack_q(q_ref, queries_ref)

    def block(b, carried):
        at = pl.ds(pl.multiple_of(b * BQ, BQ), BQ)
        shift = jnp.max(scores_of(keys, queries_ref, 0, 256, at), axis=0, keepdims=True)
        shift_ref[:, at] = shift
        set_shift(queries_ref, at, shift)
        keep_safe(keys, queries_ref, at, shift_ref, None, largest_key)
        acc_ref[:, at] = weighted(keys, queries_ref, values, at)
        return carried

    lax.fori_loop(0, HALF // BQ, block, 0)


def other_kernel(
    kv_ref, queries_in, shift_in, acc_in, pick_ref, out_ref, keys, values, queries, shift, acc, rows
):
    largest_key = unpack_kv(kv_ref, keys, values)
    queries[...] = queries_in[...]
    shift[...] = shift_in[...]
    acc[...] = acc_in[...]

    def block(b, carried):
        at = pl.ds(pl.multiple_of(b * BQ, BQ), BQ)
        keep_safe(keys, queries, at, shift, acc, largest_key)
        total = acc[:, at] + weighted(keys, queries, values, at)
        acc[:, at] = total / total[HD : HD + 1, :]
        return carried

    lax.fori_loop(0, HALF // BQ, block, 0)
    for g in range(GROUPS):
        wanted = pick_ref[g : g + 1, :]
        picked = jnp.zeros((HP, OWNERS * SLOTS), f32)
        for first, local, count in ((512 * g, 0, 512), (2048 + 256 * g, 512, 256)):
            token = lax.broadcasted_iota(jnp.int32, (count, OWNERS * SLOTS), 0) + local
            choose = jnp.where(token == wanted, 1.0, 0.0).astype(bf16)
            picked = picked + jnp.dot(
                acc[:, first : first + count].astype(bf16), choose, preferred_element_type=f32
            )
        turned = jnp.concatenate((picked, jnp.zeros((128 - HP, OWNERS * SLOTS), f32)), axis=0).T
        rows[g] = turned

    def owner(d, carried):
        at = pl.ds(pl.multiple_of(d * SLOTS, 8), SLOTS)
        out_ref[d] = jnp.concatenate([rows[g, at, :] for g in range(GROUPS)], axis=0).astype(bf16)
        return carried

    lax.fori_loop(0, OWNERS, owner, 0)


def final_kernel(
    o_ref, act_ref, slot_ref, home_ref, w_ref, bias_ref, gain_ref, shift_ref, out_ref, attended
):
    for h in range(HEADS):
        for x in range(2):
            attended[x * 96 : x * 96 + 96, h * 128 : h * 128 + 128] = o_ref[2 * h + x]
    slot = lax.broadcasted_iota(jnp.int32, (CAP, CAP), 1)
    choose = jnp.where(slot == slot_ref[:, 0:1], 1.0, 0.0).astype(bf16)
    listed_rows = jnp.dot(choose, attended[...], preferred_element_type=f32).astype(bf16)
    place = lax.broadcasted_iota(jnp.int32, (CAP, OWNERS * 8), 1)
    choose = jnp.where(place == home_ref[:, 0:1], 1.0, 0.0).astype(bf16)
    tokens = jnp.dot(choose, act_ref[...], preferred_element_type=f32)
    hidden = tokens + jnp.dot(listed_rows, w_ref[...], preferred_element_type=f32) + bias_ref[...]
    hidden = hidden.astype(bf16).astype(f32)
    normed = layer_norm(hidden, gain_ref[...], shift_ref[...])
    out_ref[0] = jnp.where(slot_ref[:, 0:1] >= 0, normed, 0.0).astype(bf16)


def routes(mask_tokens, assignment, frames, patches, me_x, me_block):
    lists = jnp.take(mask_tokens, assignment, axis=0)
    listed = lists >= 0
    token = jnp.maximum(lists, 0)
    frame, patch = token // (patches * 8), token % (patches * 8)
    z, space = frame // frames, patch // patches
    y, x = space // 2, space % 2
    local = frame % frames * patches + patch % patches
    block = z * 8 + space
    keys = jnp.concatenate(
        (
            (z * 2 + x)[:, :, None] == jnp.arange(8)[None, None, :],
            block[:, :, None] == jnp.arange(OWNERS)[None, None, :],
        ),
        axis=-1,
    ) & listed[:, :, None]
    keys = keys.astype(bf16)
    entry = jnp.arange(CAP)
    earlier = (entry[:, None] > entry[None, :]).astype(bf16)
    before = jnp.einsum("ef,dfk->dek", earlier, keys, preferred_element_type=f32) * keys.astype(f32)
    rank = jnp.sum(before[:, :, :8], axis=-1).astype(jnp.int32)
    home_rank = jnp.sum(before[:, :, 8:], axis=-1).astype(jnp.int32)
    slot = z * SLOTS + rank
    column = jnp.where(local < MAIN, y * MAIN + local, 4 * MAIN + y * (TOK - MAIN) + local - MAIN)
    mine = listed & (x == me_x)
    hit = mine[:, :, None] & (slot[:, :, None] == jnp.arange(GROUPS * SLOTS)[None, None, :])
    pick = jnp.sum(jnp.where(hit, column[:, :, None] + 1, 0), axis=1) - 1
    pick = pick.reshape(OWNERS, GROUPS, SLOTS).transpose(1, 0, 2).reshape(GROUPS, OWNERS * SLOTS)
    here = listed & (block == me_block)
    hit = here[:, :, None] & (home_rank[:, :, None] == jnp.arange(8)[None, None, :])
    act_pick = jnp.sum(jnp.where(hit, local[:, :, None] + 1, 0), axis=1) - 1

    def own(values, base):
        row = lax.dynamic_index_in_dim(jnp.where(listed, values, base), me_block, 0, keepdims=False)
        return jnp.broadcast_to(row[:, None], (CAP, 128))

    return pick, act_pick, own(x * (GROUPS * SLOTS) + slot, -1), own(block * 8 + home_rank, -1)


def local(
    activations,
    attn_gain,
    attn_shift,
    w_qkv,
    b_qkv,
    w_out,
    b_out,
    final_gain,
    final_shift,
    mask_tokens,
    assignment,
):
    frames, patches, _ = activations.shape
    tokens = activations.reshape(TOK, D)
    heads_axes = ("tm", "y")
    all_axes = ("tm", "y", "x")
    me_x = lax.axis_index("x")
    me_block = lax.axis_index("tm") * 8 + lax.axis_index("y") * 2 + me_x

    kv_out, normed = pl.pallas_call(
        kv_kernel,
        in_specs=[vmem(), vmem(), vmem(), pl.BlockSpec(memory_space=pl.ANY), vmem()],
        out_specs=[vmem(), vmem()],
        out_shape=[
            jax.ShapeDtypeStruct((HEADS, 3 * HP, 128), bf16),
            jax.ShapeDtypeStruct((TOK, D), bf16),
        ],
        scratch_shapes=[
            pltpu.VMEM((D, 2 * D), bf16),
            pltpu.VMEM((2 * D, 128), f32),
            pltpu.VMEM((2 * D, 128), f32),
            pltpu.SemaphoreType.DMA((11,)),
        ],
        compiler_params=params(40),
        cost_estimate=pl.CostEstimate(flops=2 * TOK * D * 2 * D, bytes_accessed=9 * MIB, transcendentals=0),
        name="kv_projection",
    )(tokens, attn_gain[None], attn_shift[None], w_qkv, b_qkv[None])
    kv_in = lax.all_to_all(kv_out, heads_axes, 0, 0, tiled=True)

    q_out = pl.pallas_call(
        q_kernel,
        in_specs=[vmem(), pl.BlockSpec(memory_space=pl.ANY), vmem()],
        out_specs=vmem(),
        out_shape=jax.ShapeDtypeStruct((HEADS, HP + HP // 2, 128), bf16),
        scratch_shapes=[
            pltpu.VMEM((D, D), bf16),
            pltpu.VMEM((D, 128), f32),
            pltpu.VMEM((D, 128), f32),
            pltpu.SemaphoreType.DMA((6,)),
        ],
        compiler_params=params(24),
        cost_estimate=pl.CostEstimate(flops=2 * TOK * D * D, bytes_accessed=5 * MIB, transcendentals=0),
        name="q_projection",
    )(normed, w_qkv, b_qkv[None])
    q_out, kv_in = lax.optimization_barrier((q_out, kv_in))
    q_in = lax.all_to_all(q_out, heads_axes, 0, 0, tiled=True)
    kv_other = lax.ppermute(kv_in, "x", [(0, 1), (1, 0)])

    pick, act_pick, slot, home = routes(mask_tokens, assignment, frames, patches, me_x, me_block)
    w_padded = jnp.pad(w_out.reshape(HEADS, HD, D), ((0, 0), (0, 128 - HD), (0, 0))).reshape(HEADS * 128, D)
    act_choose = (act_pick.reshape(OWNERS * 8, 1) == jnp.arange(TOK)[None, :]).astype(bf16)
    act_out = jnp.dot(act_choose, tokens, preferred_element_type=f32).astype(bf16)
    act_out = act_out.reshape(OWNERS, 8, D)

    attend_cost = pl.CostEstimate(
        flops=4 * HALF * HALF * 256, bytes_accessed=8 * MIB, transcendentals=HALF * HALF
    )
    queries, shift, acc = pl.pallas_call(
        own_kernel,
        in_specs=[vmem(), vmem()],
        out_specs=[vmem(), vmem(), vmem()],
        out_shape=[
            jax.ShapeDtypeStruct((256, HALF), bf16),
            jax.ShapeDtypeStruct((1, HALF), f32),
            jax.ShapeDtypeStruct((HP, HALF), f32),
        ],
        scratch_shapes=[pltpu.VMEM((HALF, 256), bf16), pltpu.VMEM((HP, HALF), bf16)],
        compiler_params=params(56),
        cost_estimate=attend_cost,
        name="attend_own",
    )(q_in, kv_in)

    act_out, q_in = lax.optimization_barrier((act_out, q_in))
    act_in = lax.all_to_all(act_out, all_axes, 0, 0, tiled=True)

    o_out = pl.pallas_call(
        other_kernel,
        in_specs=[vmem()] * 5,
        out_specs=vmem(),
        out_shape=jax.ShapeDtypeStruct((OWNERS, GROUPS * SLOTS, 128), bf16),
        scratch_shapes=[
            pltpu.VMEM((HALF, 256), bf16),
            pltpu.VMEM((HP, HALF), bf16),
            pltpu.VMEM((256, HALF), bf16),
            pltpu.VMEM((1, HALF), f32),
            pltpu.VMEM((HP, HALF), f32),
            pltpu.VMEM((GROUPS, OWNERS * SLOTS, 128), f32),
        ],
        compiler_params=params(58),
        cost_estimate=attend_cost,
        name="attend_other",
    )(kv_other, queries, shift, acc, pick)
    o_in = lax.all_to_all(o_out, all_axes, 0, 0, tiled=True)

    return pl.pallas_call(
        final_kernel,
        in_specs=[vmem()] * 8,
        out_specs=vmem(),
        out_shape=jax.ShapeDtypeStruct((1, CAP, D), bf16),
        scratch_shapes=[pltpu.VMEM((CAP, HEADS * 128), bf16)],
        compiler_params=params(40),
        cost_estimate=pl.CostEstimate(flops=2 * TOK * D * D, bytes_accessed=10 * MIB, transcendentals=0),
        name="finish",
    )(
        o_in,
        act_in.reshape(OWNERS * 8, D),
        slot,
        home,
        w_padded,
        b_out[None],
        final_gain[None],
        final_shift[None],
    )


def solution(mesh):
    times, spaces, clips = (mesh.shape[a] for a in ("tm", "space", "clip"))
    fine = Mesh(mesh.devices.reshape(times, spaces // 2, 2, clips), ("tm", "y", "x", "clip"))
    in_specs = (
        P(("clip", "tm"), ("y", "x"), None),
        P(),
        P(),
        P(),
        P(),
        P(),
        P(),
        P(),
        P(),
        P("clip", None),
        P("clip"),
    )
    out_specs = P(("clip", "tm", "y", "x"), None, None)
    return jax.shard_map(local, mesh=fine, in_specs=in_specs, out_specs=out_specs, check_vma=False)
```

time: 276 us -> 144 us (0.52)
  matrix products: 91.7 us -> 1.75 us
  Pallas kernels: 0 us -> 67.8 us
  local copies, waits for them, and re-layouts: 70.4 us -> 21.5 us
  blocking collectives: 21.5 us -> 0 us
  other arithmetic: 24.7 us -> 5.17 us
  between operations: 14 us -> 0.34 us
  waiting for transfers between devices: 32.5 us -> 20.1 us
  starting transfers between devices: 19.5 us -> 26.1 us
    dot_general x34 -> x2, matrix products: 91.7 us -> 1.75 us  [the longest x1 1.27 us: local(): jnp.dot(act_choose, tokens, preferred_element_type=f32).astype(bf16)]
    pallas_call x0 -> x5, Pallas kernels: none -> 67.8 us  [the longest x1 26.3 us: local(): pl.pallas_call(other_kernel, in_specs=[vmem()] * 5, out_specs=vmem(), out...]
    all_to_all x1 -> x0, blocking collectives: 21.5 us -> none  [items_in_groups(): lax.all_to_all(group, axis, split_axis=split_dim, concat_axis=concat_dim,...]
    while x48 -> x0, local copies, waits for them, and re-layouts: 20.2 us -> none
    slice x12 -> x0, local copies, waits for them, and re-layouts: 17.7 us -> none  [the longest x3 14.5 us: items_in_groups(): lax.slice_in_dim(a, k * (items // count), (k + 1) * (items // count), axi...]
    another operation x8 -> x0, local copies, waits for them, and re-layouts: 13.5 us -> none  [the longest x4 12.7 us: local(): jnp.stack((query_rows, paired[0], paired[1]))]
    reduce_sum x21 -> x4, other arithmetic: 16 us -> 4.26 us  [the longest x1 3.43 us: routes(): pick = jnp.sum(jnp.where(hit, column[:, :, None] + 1, 0), axis=1) - 1]
    all_to_all x4, waiting for transfers between devices: 27.9 us -> 20.1 us  [the longest x1 8.02 us: local(): o_in = lax.all_to_all(o_out, all_axes, 0, 0, tiled=True)]
  transfers between devices with their start and end apart: 6 -> 5, of which waited for: 4 -> 3; matrix products, arithmetic and copies ran while one was open for 42% -> 10% of each run, Pallas kernels for 0% -> 40%
where the time goes in v1:
time: 144 us; the launch traced here: 143 us
  Pallas kernels  67.8 us (47%)
  starting transfers between devices  26.1 us (18%)
  local copies, waits for them, and re-layouts  21.5 us (15%)
  waiting for transfers between devices  20.1 us (14%)
  other arithmetic  5.17 us (4%)
  matrix products  1.75 us (1%)
    pallas_call x1, Pallas kernels, local(): pl.pallas_call(other_kernel, in_specs=[vmem()] * 5, out_specs=vmem(), out...  26.3 us
    pallas_call x1, Pallas kernels, local(): pl.pallas_call(own_kernel, in_specs=[vmem(), vmem()], out_specs=[vmem(),...  26.1 us
    unnamed x24, local copies, waits for them, and re-layouts  12.5 us
    all_to_all x1, starting transfers between devices, local(): o_in = lax.all_to_all(o_out, all_axes, 0, 0, tiled=True)  8.26 us
    all_to_all x1, starting transfers between devices, local(): kv_in = lax.all_to_all(kv_out, heads_axes, 0, 0, tiled=True)  8.14 us
    all_to_all x1, waiting for transfers between devices, local(): o_in = lax.all_to_all(o_out, all_axes, 0, 0, tiled=True)  8.02 us
    pallas_call x1, Pallas kernels, local(): pl.pallas_call(kv_kernel, in_specs=[vmem(), vmem(), vmem(), pl.BlockSpec(...  7.98 us
    all_to_all x1, waiting for transfers between devices, local(): kv_in = lax.all_to_all(kv_out, heads_axes, 0, 0, tiled=True)  7.38 us
  transfers between devices with their start and end apart: 5, of which 3 were waited for; matrix products, arithmetic and copies ran while one was open for 10% of the time, Pallas kernels for 40%

profile of v1, /device:TPU:0, one launch (start us, length us, event | category | flops | bytes accessed | tf_op | source)
XLA Modules:
  0.0 142.9 jit_solution(3967259020620951199)
XLA Ops:
  0.0 0.7 broadcast_in_dim.90.gain_ref
  0.7 0.7 broadcast_in_dim.91.shift_ref
  1.4 0.7 broadcast_in_dim.92.bias_ref
  2.2 4.4 %copy-done.1 = bf16[1408,4224]{1,0:T(8,128)(2,1)S(1)} copy-done((bf16[1408,4224]{1,0:T(8,128)(2,1)S(1)}, bf16[1408,4224]{1,0:T(8,128)(2,1)}, u32[]{:S(2)}) %copy-start.1) | copy-done | bytes 11894808
  6.5 1.0 copy-done.4
  7.6 8.0 %kv_projection.1 = (bf16[16,288,128]{2,1,0:T(8,128)(2,1)}, bf16[192,1408]{1,0:T(8,128)(2,1)S(1)}) custom-call(bf16[192,1408]{1,0:T(8,128)(2,1)S(1)} %bitcast.19, f32[1,1408]{1,0:T(1,128)S(1)} %broadcast_in_dim.90.gain_ref, f32[1,1408]{1,0:T(1,128)S(1)} %broadcast_in_dim.91.shift_ref, bf16[1408,4224]{1,0:T(8,128)(2,1)S(1)} %copy-done.1, ...), custom_call_target="tpu_custom_call" | custom-call | flops 1522532352 | bytes 9437184 | tf_op jit(solution)/shard_map/kv_projection/pallas_call | solution.py:336
  15.6 8.1 %all-to-all-start = ((bf16[16,288,128]{2,1,0:T(8,128)(2,1)}), bf16[16,288,128]{2,1,0:T(8,128)(2,1)S(1)}, u32[]{:S(2)}, u32[]{:S(2)}) async-start(bf16[16,288,128]{2,1,0:T(8,128)(2,1)} %get-tuple-element.14), calls=%async_computation | async-start | bytes 2359296 | tf_op jit(solution)/shard_map/all_to_all | solution.py:354
  26.6 4.4 %copy-done.2 = bf16[1408,4224]{1,0:T(8,128)(2,1)S(1)} copy-done((bf16[1408,4224]{1,0:T(8,128)(2,1)S(1)}, bf16[1408,4224]{1,0:T(8,128)(2,1)}, u32[]{:S(2)}) %copy-start.2) | copy-done | bytes 11894808
  31.0 4.4 %q_projection.1 = bf16[16,144,128]{2,1,0:T(8,128)(2,1)} custom-call(bf16[192,1408]{1,0:T(8,128)(2,1)S(1)} %get-tuple-element.13.normed_ref, bf16[1408,4224]{1,0:T(8,128)(2,1)S(1)} %copy-done.2, f32[1,4224]{1,0:T(1,128)S(1)} %broadcast_in_dim.92.bias_ref), custom_call_target="tpu_custom_call" | custom-call | flops 761266176 | bytes 5242880 | tf_op jit(solution)/shard_map/q_projection/pallas_call | solution.py:356
  35.6 7.4 %all-to-all-done.kv_ref = bf16[16,288,128]{2,1,0:T(8,128)(2,1)S(1)} async-done(((bf16[16,288,128]{2,1,0:T(8,128)(2,1)}), bf16[16,288,128]{2,1,0:T(8,128)(2,1)S(1)}, u32[]{:S(2)}, u32[]{:S(2)}) %all-to-all-start) | async-done | bytes 1179680 | tf_op jit(solution)/shard_map/all_to_all | solution.py:354
  43.0 3.6 %all-to-all-start.1 = ((bf16[16,144,128]{2,1,0:T(8,128)(2,1)}), bf16[16,144,128]{2,1,0:T(8,128)(2,1)S(1)}, u32[]{:S(2)}, u32[]{:S(2)}) async-start(bf16[16,144,128]{2,1,0:T(8,128)(2,1)} %q_projection.1), calls=%async_computation.1 | async-start | bytes 1179648 | tf_op jit(solution)/shard_map/all_to_all | solution.py:372
  46.6 3.4 %select_reduce_fusion = s32[32,96]{1,0:T(8,128)S(1)} fusion(s32[32,192]{1,0:T(8,128)S(1)} %select_add_fusion, s32[32,192]{1,0:T(8,128)S(1)} %get-tuple-element.28, pred[32,192]{1,0:T(8,128)(4,1)S(1)} %get-tuple-element.26), kind=kLoop, calls=%fused_computation.1 | loop fusion | flops 2356224 | bytes 67584 | tf_op jit(solution)/shard_map/reduce_sum | solution.py:303
  50.0 1.6 %collective-permute-start = (bf16[16,288,128]{2,1,0:T(8,128)(2,1)S(1)}, bf16[16,288,128]{2,1,0:T(8,128)(2,1)}, u32[]{:S(2)}, u32[]{:S(2)}) collective-permute-start(bf16[16,288,128]{2,1,0:T(8,128)(2,1)S(1)} %all-to-all-done.kv_ref), channel_id=1, source_target_pairs={{0,4},{4,0},{1,5},{5,1},{2,6},{6,2},{3,7},{7,3},{8,12},{12,8},{9,1... | collective-permute-start | bytes 3538952 | tf_op jit(solution)/shard_map/ppermute | solution.py:373
  51.7 0.7 reshape.272.pick_ref
  52.4 1.3 fusion.1
  53.7 4.7 %all-to-all-done.1.q_ref = bf16[16,144,128]{2,1,0:T(8,128)(2,1)S(1)} async-done(((bf16[16,144,128]{2,1,0:T(8,128)(2,1)}), bf16[16,144,128]{2,1,0:T(8,128)(2,1)S(1)}, u32[]{:S(2)}, u32[]{:S(2)}) %all-to-all-start.1) | async-done | bytes 589856 | tf_op jit(solution)/shard_map/all_to_all | solution.py:372
  58.4 4.6 %all-to-all-start.3 = ((bf16[32,8,1408]{2,1,0:T(8,128)(2,1)}), bf16[32,8,1408]{2,1,0:T(8,128)(2,1)S(1)}, u32[]{:S(2)}, u32[]{:S(2)}) async-start(bf16[32,8,1408]{2,1,0:T(8,128)(2,1)} %fusion.1), calls=%async_computation.3 | async-start | bytes 1441792 | tf_op jit(solution)/shard_map/all_to_all | solution.py:400
  63.0 26.1 %attend_own.1 = (bf16[256,3072]{1,0:T(8,128)(2,1)}, f32[1,3072]{1,0:T(1,128)}, f32[96,3072]{1,0:T(8,128)}) custom-call(bf16[16,144,128]{2,1,0:T(8,128)(2,1)} %copy-done.7, bf16[16,288,128]{2,1,0:T(8,128)(2,1)} %copy-done.6), custom_call_target="tpu_custom_call" | custom-call | flops 9663676416 | bytes 8388608 | tf_op jit(solution)/shard_map/attend_own/pallas_call | solution.py:384
  89.0 26.3 %attend_other.1 = bf16[32,96,128]{2,1,0:T(8,128)(2,1)} custom-call(bf16[16,288,128]{2,1,0:T(8,128)(2,1)} %collective-permute-done.kv_ref, bf16[256,3072]{1,0:T(8,128)(2,1)} %get-tuple-element.17.queries_in, f32[1,3072]{1,0:T(1,128)} %get-tuple-element.18.shift_in, f32[96,3072]{1,0:T(8,128)} %get-tuple-element.19.acc_in, s32[4,768]{1,0:T(4,128)} %reshape.272.pick_ref), custom_call_target="tpu_custom_call" | custom-call | flops 9663676416 | bytes 8388608 | tf_op jit(solution)/shard_map/attend_other/pallas_call | solution.py:402
  115.4 8.3 %all-to-all-start.2 = ((bf16[32,96,128]{2,1,0:T(8,128)(2,1)}), bf16[32,96,128]{2,1,0:T(8,128)(2,1)S(1)}, u32[]{:S(2)}, u32[]{:S(2)}) async-start(bf16[32,96,128]{2,1,0:T(8,128)(2,1)} %attend_other.1), calls=%async_computation.2 | async-start | bytes 1572864 | tf_op jit(solution)/shard_map/all_to_all | solution.py:419
  123.7 5.3 %pad.4 = bf16[16,128,1408]{2,1,0:T(8,128)(2,1)} pad(bf16[16,88,1408]{2,1,0:T(8,128)(2,1)} %bitcast.21, bf16[]{:T(256)} %constant.158.clone.1), padding=0_0x0_40x0_0 | pad | bytes 9732098 | tf_op jit(solution)/shard_map/jit(_pad)/pad | solution.py:376
  129.0 8.0 %all-to-all-done.2.o_ref = bf16[32,96,128]{2,1,0:T(8,128)(2,1)S(1)} async-done(((bf16[32,96,128]{2,1,0:T(8,128)(2,1)}), bf16[32,96,128]{2,1,0:T(8,128)(2,1)S(1)}, u32[]{:S(2)}, u32[]{:S(2)}) %all-to-all-start.2) | async-done | bytes 786464 | tf_op jit(solution)/shard_map/all_to_all | solution.py:419
  137.2 2.6 %copy-done.3 = bf16[16,128,1408]{2,1,0:T(8,128)(2,1)S(1)} copy-done((bf16[16,128,1408]{2,1,0:T(8,128)(2,1)S(1)}, bf16[16,128,1408]{2,1,0:T(8,128)(2,1)}, u32[]{:S(2)}) %copy-start.3) | copy-done | bytes 5767192
  139.8 3.1 %finish.1 = bf16[1,192,1408]{2,1,0:T(8,128)(2,1)} custom-call(bf16[32,96,128]{2,1,0:T(8,128)(2,1)S(1)} %all-to-all-done.2.o_ref, bf16[256,1408]{1,0:T(8,128)(2,1)S(1)} %bitcast.18, s32[192,128]{1,0:T(8,128)S(1)} %broadcast_in_dim.101.slot_ref, s32[192,128]{1,0:T(8,128)S(1)} %broadcast_in_dim.103.home_ref, bf16[2048,1408]{1,0:T(8,128)(2,1)S(1)} %bitcast.17, ...), custom_call_target="tpu_custom_call" | custom-call | flops 761266176 | bytes 10485760 | tf_op jit(solution)/shard_map/finish/pallas_call | solution.py:421
  (49 shorter events, 3.2 us)
Async XLA Ops:
  0.0 23.8 %copy-start = (s32[32,192]{1,0:T(8,128)S(1)}, s32[32,192]{1,0:T(8,128)}, u32[]{:S(2)}) copy-start(s32[32,192]{1,0:T(8,128)} %param.20) | copy-start | bytes 73732
  2.2 4.4 %copy-start.1 = (bf16[1408,4224]{1,0:T(8,128)(2,1)S(1)}, bf16[1408,4224]{1,0:T(8,128)(2,1)}, u32[]{:S(2)}) copy-start(bf16[1408,4224]{1,0:T(8,128)(2,1)} %w_ref.3) | copy-start | bytes 35684356
  6.5 1.0 copy-start.4
  15.6 8.2 %copy-start.11 = (s32[32]{0:T(128)S(1)}, s32[32]{0:T(128)}, u32[]{:S(2)}) copy-start(s32[32]{0:T(128)} %param.21) | copy-start | bytes 388
  15.6 27.4 %all-to-all-start = ((bf16[16,288,128]{2,1,0:T(8,128)(2,1)}), bf16[16,288,128]{2,1,0:T(8,128)(2,1)S(1)}, u32[]{:S(2)}, u32[]{:S(2)}) async-start(bf16[16,288,128]{2,1,0:T(8,128)(2,1)} %get-tuple-element.14), calls=%async_computation | async-start | bytes 2359296 | tf_op jit(solution)/shard_map/all_to_all | solution.py:354
  26.6 4.4 %copy-start.2 = (bf16[1408,4224]{1,0:T(8,128)(2,1)S(1)}, bf16[1408,4224]{1,0:T(8,128)(2,1)}, u32[]{:S(2)}) copy-start(bf16[1408,4224]{1,0:T(8,128)(2,1)} %w_ref.3) | copy-start | bytes 35684356
  35.4 16.9 %copy-start.5 = (bf16[6,32,1408]{2,1,0:T(8,128)(2,1)S(1)}, bf16[6,32,1408]{2,1,0:T(8,128)(2,1)}, u32[]{:S(2)}) copy-start(bf16[6,32,1408]{2,1,0:T(8,128)(2,1)} %param.11) | copy-start | bytes 1622020
  43.0 15.4 %copy-start.6 = (bf16[16,288,128]{2,1,0:T(8,128)(2,1)}, bf16[16,288,128]{2,1,0:T(8,128)(2,1)S(1)}, u32[]{:S(2)}) copy-start(bf16[16,288,128]{2,1,0:T(8,128)(2,1)S(1)} %all-to-all-done.kv_ref) | copy-start | bytes 3538948
  43.0 15.4 %all-to-all-start.1 = ((bf16[16,144,128]{2,1,0:T(8,128)(2,1)}), bf16[16,144,128]{2,1,0:T(8,128)(2,1)S(1)}, u32[]{:S(2)}, u32[]{:S(2)}) async-start(bf16[16,144,128]{2,1,0:T(8,128)(2,1)} %q_projection.1), calls=%async_computation.1 | async-start | bytes 1179648 | tf_op jit(solution)/shard_map/all_to_all | solution.py:372
  50.0 39.0 %collective-permute-start = (bf16[16,288,128]{2,1,0:T(8,128)(2,1)S(1)}, bf16[16,288,128]{2,1,0:T(8,128)(2,1)}, u32[]{:S(2)}, u32[]{:S(2)}) collective-permute-start(bf16[16,288,128]{2,1,0:T(8,128)(2,1)S(1)} %all-to-all-done.kv_ref), channel_id=1, source_target_pairs={{0,4},{4,0},{1,5},{5,1},{2,6},{6,2},{3,7},{7,3},{8,12},{12,8},{9,1... | collective-permute-start | bytes 3538952 | tf_op jit(solution)/shard_map/ppermute | solution.py:373
  58.4 4.6 %copy-start.7 = (bf16[16,144,128]{2,1,0:T(8,128)(2,1)}, bf16[16,144,128]{2,1,0:T(8,128)(2,1)S(1)}, u32[]{:S(2)}) copy-start(bf16[16,144,128]{2,1,0:T(8,128)(2,1)S(1)} %all-to-all-done.1.q_ref) | copy-start | bytes 1769476
  58.4 57.0 %all-to-all-start.3 = ((bf16[32,8,1408]{2,1,0:T(8,128)(2,1)}), bf16[32,8,1408]{2,1,0:T(8,128)(2,1)S(1)}, u32[]{:S(2)}, u32[]{:S(2)}) async-start(bf16[32,8,1408]{2,1,0:T(8,128)(2,1)} %fusion.1), calls=%async_computation.3 | async-start | bytes 1441792 | tf_op jit(solution)/shard_map/all_to_all | solution.py:400
  115.3 8.3 %copy-start.8 = (f32[1408]{0:T(1024)S(1)}, f32[1408]{0:T(1024)}, u32[]{:S(2)}) copy-start(f32[1408]{0:T(1024)} %param.17) | copy-start | bytes 16900
  115.3 8.3 %copy-start.9 = (f32[1408]{0:T(1024)S(1)}, f32[1408]{0:T(1024)}, u32[]{:S(2)}) copy-start(f32[1408]{0:T(1024)} %param.18) | copy-start | bytes 16900
  115.3 8.3 %copy-start.10 = (f32[1408]{0:T(1024)S(1)}, f32[1408]{0:T(1024)}, u32[]{:S(2)}) copy-start(f32[1408]{0:T(1024)} %param.19) | copy-start | bytes 16900
  115.4 21.6 %all-to-all-start.2 = ((bf16[32,96,128]{2,1,0:T(8,128)(2,1)}), bf16[32,96,128]{2,1,0:T(8,128)(2,1)S(1)}, u32[]{:S(2)}, u32[]{:S(2)}) async-start(bf16[32,96,128]{2,1,0:T(8,128)(2,1)} %attend_other.1), calls=%async_computation.2 | async-start | bytes 1572864 | tf_op jit(solution)/shard_map/all_to_all | solution.py:419
  137.2 2.6 %copy-start.3 = (bf16[16,128,1408]{2,1,0:T(8,128)(2,1)S(1)}, bf16[16,128,1408]{2,1,0:T(8,128)(2,1)}, u32[]{:S(2)}) copy-start(bf16[16,128,1408]{2,1,0:T(8,128)(2,1)} %pad.4) | copy-start | bytes 17301508

commit v2 on v0

v2 whole, which is shorter than its diff:
```python
import functools
import math

import jax
import jax.numpy as jnp
from jax import lax
from jax.experimental import pallas as pl
from jax.experimental.pallas import tpu as pltpu
from jax.sharding import Mesh
from jax.sharding import PartitionSpec as P

EPSILON = 1e-06
D = 1408
HEADS = 16
HD = 88
HP = 96
TOK = 192
MAIN = 128
OWNERS = 32
BLOCKS = 32
CAP = 192
EACH = 6
PART = 96
TOKENS = BLOCKS * TOK
COLUMNS = BLOCKS * PART
QROWS = 72
ROWS = 3 * HD + QROWS
GROUPS = 4
SLOTS = 24
WINDOW = 8 * PART + 128
BQ = 512
BK = 2048
QK_SCALE = math.log2(math.e) / math.sqrt(HD)
SAFE = 90.0
MIB = 1 << 20

f32 = jnp.float32
bf16 = jnp.bfloat16


def params(vmem_mib):
    return pltpu.CompilerParams(vmem_limit_bytes=vmem_mib * MIB)


def vmem():
    return pl.BlockSpec(memory_space=pltpu.VMEM)


def layer_norm(values, ln_gain, ln_shift):
    centre = jnp.mean(values, axis=-1, keepdims=True)
    deviation = values - centre
    variance = jnp.mean(deviation * deviation, axis=-1, keepdims=True)
    return deviation * lax.rsqrt(variance + EPSILON) * ln_gain + ln_shift


def lanes_below(shape, bound):
    return lax.broadcasted_iota(jnp.int32, shape, 1) < bound


def where_tokens(lists):
    token = jnp.maximum(lists, 0)
    frame, patch = token >> 8, token & 255
    z = (frame * 43) >> 8
    return z * 8 + (patch >> 5), (frame - z * 6) * 32 + (patch & 31)


def ones_where(condition):
    return jnp.where(condition, 1.0, 0.0)


def query_choice(lists, me):
    block, local = where_tokens(lists)
    mine = ones_where((lists >= 0) & (block == me))
    upper = ones_where(
        lax.broadcasted_iota(jnp.int32, (CAP, CAP), 0) < lax.broadcasted_iota(jnp.int32, (CAP, CAP), 1)
    )
    rank = jnp.dot(mine.astype(bf16), upper.astype(bf16), preferred_element_type=f32)
    count = jnp.sum(mine, axis=1, keepdims=True)
    lower = ones_where(
        lax.broadcasted_iota(jnp.int32, (OWNERS, OWNERS), 0)
        > lax.broadcasted_iota(jnp.int32, (OWNERS, OWNERS), 1)
    ).astype(bf16)
    bases = []
    for part in range(2):
        held = jnp.zeros_like(count)
        for k in range(part, EACH, 2):
            held = held + ones_where(count > k)
        held = jnp.broadcast_to(held, (OWNERS, 128)).astype(bf16)
        bases.append(jnp.dot(lower, held, preferred_element_type=f32)[:, 0:1] + part * PART)
    lane = lax.broadcasted_iota(jnp.int32, (OWNERS, CAP), 1).astype(f32)
    slots, tokens = [], []
    for k in range(EACH):
        token = jnp.sum(jnp.where(rank == k, mine * local.astype(f32), 0.0), axis=1, keepdims=True)
        have = count > k
        slots.append(ones_where(have & (lane == bases[k % 2] + k // 2)))
        tokens.append(ones_where(have & (lane == token)))
    return lax.dot_general(
        jnp.concatenate(slots, axis=0).astype(bf16),
        jnp.concatenate(tokens, axis=0).astype(bf16),
        (((0,), (0,)), ((), ())),
        preferred_element_type=f32,
    ).astype(bf16)


def qkv_kernel(
    me_ref, x_ref, gain_ref, shift_ref, lists_ref, w_ref, bias_ref, out_ref, buffer, main, rest, asked, sems
):
    copies = [
        pltpu.make_async_copy(w_ref.at[:, pl.ds(at, D)], buffer.at[:, pl.ds(at, D)], sems.at[i])
        for i, at in enumerate((D, 2 * D, 0))
    ]
    for copy in copies:
        copy.start()
    normed = layer_norm(x_ref[...].astype(f32), gain_ref[...][None], shift_ref[...][None]).astype(bf16)
    chosen = jnp.dot(query_choice(lists_ref[...], me_ref[0]), normed, preferred_element_type=f32)
    chosen = chosen.astype(bf16)
    for copy, at, rows in zip(copies, (D, 2 * D, 0), (normed, normed, chosen)):
        copy.wait()
        part = jnp.dot(rows, buffer[:, at : at + D], preferred_element_type=f32)
        part = (part + bias_ref[at : at + D][None]).astype(bf16).astype(f32)
        if at == 0:
            for x in range(2):
                half = part[x * PART : x * PART + PART]
                asked[x] = jnp.concatenate((half, half[:32]), axis=0).T
        else:
            tail = part[MAIN:]
            main[at - D : at, :] = part[:MAIN].T
            rest[at - D : at, :] = jnp.concatenate((tail, tail), axis=0).T
    low = lanes_below((HD, 128), 64)
    queries = lanes_below((QROWS, 128), PART)
    for h in range(HEADS):
        k_rows, v_rows = slice(h * HD, h * HD + HD), slice(D + h * HD, D + h * HD + HD)
        both = jnp.where(low, rest[k_rows, :], rest[v_rows, :])
        for x in range(2):
            top = asked[x, h * HD : h * HD + QROWS, :]
            last = jnp.concatenate(
                (asked[x, h * HD + QROWS : h * HD + HD, :], jnp.zeros((8, 128), f32)), axis=0
            )
            spread = jnp.concatenate((last, pltpu.roll(last, 64, 1), pltpu.roll(last, 32, 1)), axis=0)
            out_ref[2 * h + x] = jnp.concatenate(
                (main[k_rows, :], main[v_rows, :], both, jnp.where(queries, top, spread)), axis=0
            ).astype(bf16)


def unpack_pair(first, second):
    low = lanes_below(first.shape, 64)
    return (
        jnp.where(low, first, pltpu.roll(second, 64, 1)),
        jnp.where(low, pltpu.roll(first, 64, 1), second),
    )


def put_keys(tile, k_tile, v_tile, keys, values):
    at = pl.ds(pl.multiple_of(tile * 128, 128), 128)
    ones = jnp.ones((HP - HD, 128), f32)
    turned = jnp.concatenate((k_tile, ones, jnp.zeros((128 - HP, 128), f32)), axis=0).T.astype(bf16)
    keys[at, 0:128] = turned
    keys[at, 128:256] = turned
    values[:, at] = jnp.concatenate((v_tile, ones), axis=0).astype(bf16)
    return jnp.sum(k_tile * k_tile, axis=0, keepdims=True)


def put_queries(packed, first, count, columns):
    shape = (HD - QROWS, 128)
    parts = [
        pltpu.roll(packed[24 * i : 24 * i + HD - QROWS], 32 * (i + 1), 1) for i in range(3)
    ]
    last = jnp.where(lanes_below(shape, 32), parts[0], jnp.where(lanes_below(shape, 64), parts[1], parts[2]))
    whole = jnp.concatenate((packed, last), axis=0)
    lane = lax.broadcasted_iota(jnp.int32, whole.shape, 1)
    turn = first & 127
    turned = pltpu.roll(jnp.where(lane < count, whole, 0.0), turn, 1)
    at = pl.ds(pl.multiple_of((first >> 7) * 128, 128), 128)
    columns[:, at] = columns[:, at] + jnp.where(lane >= turn, turned, 0.0)
    at = pl.ds(pl.multiple_of((first >> 7) * 128 + 128, 128), 128)
    columns[:, at] = jnp.where(lane < turn, turned, 0.0)


def set_shift(queries, at, shift):
    high = shift.astype(bf16).astype(f32)
    middle = (shift - high).astype(bf16).astype(f32)
    low = shift - high - middle
    row = lax.broadcasted_iota(jnp.int32, (8, shift.shape[1]), 0)
    rows = jnp.where(row == 0, -high, jnp.where(row == 1, -middle, jnp.where(row == 2, -low, 0.0)))
    old = queries[HP - 16 : HP, at].astype(f32)
    queries[HP - 16 : HP, at] = jnp.concatenate((old[:8], rows), axis=0).astype(bf16)


def scores_of(keys, queries, first, count, at):
    return jnp.dot(keys[pl.ds(first, count), :], queries[:, at], preferred_element_type=f32)


def attend_columns(start, width, columns, queries, keys, values, acc, largest_key):
    at = pl.ds(pl.multiple_of(start, 256), width)
    scaled = columns[:, at] * QK_SCALE
    high = scaled.astype(bf16).astype(f32)
    zeros = jnp.zeros((128 - HD, width), f32)
    here = pl.ds(0, width)
    queries[0:128, here] = jnp.concatenate((high, zeros), axis=0).astype(bf16)
    queries[128:256, here] = jnp.concatenate((scaled - high, zeros), axis=0).astype(bf16)
    shift = jnp.max(scores_of(keys, queries, 0, 128, here), axis=0, keepdims=True)
    set_shift(queries, here, shift)
    norm = jnp.sqrt(jnp.sum(scaled * scaled, axis=0, keepdims=True) * largest_key)

    @pl.when(jnp.logical_not(jnp.max(norm * 1.01 - shift) <= SAFE))
    def _():
        def step(i, above):
            got = scores_of(keys, queries, pl.multiple_of(i * 256, 256), 256, here)
            return jnp.maximum(above, jnp.max(got, axis=0, keepdims=True))

        above = lax.fori_loop(0, TOKENS // 256, step, jnp.zeros((1, width), f32))
        set_shift(queries, here, shift + above)

    total = jnp.zeros((HP, width), f32)
    for first in range(0, TOKENS, BK):
        weights = jnp.exp2(scores_of(keys, queries, first, BK, here)).astype(bf16)
        total = total + jnp.dot(values[:, first : first + BK], weights, preferred_element_type=f32)
    acc[:, at] = total / total[HD : HD + 1, :]


def attend_kernel(first_ref, in_ref, pick_ref, out_ref, keys, values, columns, queries, acc, rows):
    columns[:, 0:128] = jnp.zeros((HD, 128), f32)

    def pair(p, largest):
        rests = []
        for j in range(2):
            block = 2 * p + j
            whole = in_ref[block].astype(f32)
            square = put_keys(block, whole[0:HD], whole[HD : 2 * HD], keys, values)
            largest = jnp.maximum(largest, square)
            rests.append(whole[2 * HD : 3 * HD])
            first = first_ref[block]
            put_queries(whole[3 * HD :], first, first_ref[block + 1] - first, columns)
        square = put_keys(BLOCKS + p, *unpack_pair(*rests), keys, values)
        return jnp.maximum(largest, square)

    largest = lax.fori_loop(0, BLOCKS // 2, pair, jnp.zeros((1, 128), f32))
    largest_key = jnp.max(largest, axis=1, keepdims=True)

    total = first_ref[BLOCKS]
    used = (total >> 7) * 128 + 128

    def clear(i, carried):
        columns[:, pl.ds(pl.multiple_of(used + i * 128, 128), 128)] = jnp.zeros((HD, 128), f32)
        return carried

    lax.fori_loop(0, 4, clear, 0)
    acc[...] = jnp.zeros_like(acc)
    blocks = (total + 255) >> 9

    def block(b, carried):
        attend_columns(b * BQ, BQ, columns, queries, keys, values, acc, largest_key)
        return carried

    lax.fori_loop(0, blocks, block, 0)

    @pl.when(total > blocks * BQ)
    def _():
        attend_columns(blocks * BQ, 256, columns, queries, keys, values, acc, largest_key)

    for g in range(GROUPS):
        begin = pl.multiple_of((first_ref[8 * g] >> 7) * 128, 128)
        near = lax.broadcasted_iota(jnp.int32, (WINDOW, OWNERS * SLOTS), 0)
        choose = ones_where(near == pick_ref[g : g + 1, :]).astype(bf16)
        picked = jnp.dot(acc[:, pl.ds(begin, WINDOW)].astype(bf16), choose, preferred_element_type=f32)
        rows[g] = jnp.concatenate((picked, jnp.zeros((128 - HP, OWNERS * SLOTS), f32)), axis=0).T

    def owner(d, carried):
        at = pl.ds(pl.multiple_of(d * SLOTS, 8), SLOTS)
        out_ref[d] = jnp.concatenate([rows[g, at, :] for g in range(GROUPS)], axis=0).astype(bf16)
        return carried

    lax.fori_loop(0, OWNERS, owner, 0)


def final_kernel(
    o_ref, act_ref, slot_ref, home_ref, w_ref, bias_ref, gain_ref, shift_ref, out_ref, attended
):
    for h in range(HEADS):
        for x in range(2):
            attended[x * 96 : x * 96 + 96, h * 128 : h * 128 + 128] = o_ref[2 * h + x]
    slot = lax.broadcasted_iota(jnp.int32, (CAP, CAP), 1)
    choose = jnp.where(slot == slot_ref[:, 0:1], 1.0, 0.0).astype(bf16)
    listed_rows = jnp.dot(choose, attended[...], preferred_element_type=f32)
    place = lax.broadcasted_iota(jnp.int32, (CAP, OWNERS * 8), 1)
    choose = jnp.where(place == home_ref[:, 0:1], 1.0, 0.0).astype(bf16)
    tokens = jnp.dot(choose, act_ref[...], preferred_element_type=f32)
    hidden = tokens + bias_ref[...][None]
    low = lanes_below((CAP, 128), HD)
    for p in range(HEADS // 2):
        first = listed_rows[:, p * 256 : p * 256 + 128]
        second = pltpu.roll(listed_rows[:, p * 256 + 128 : p * 256 + 256], HD, 1)
        both = jnp.concatenate((jnp.where(low, first, second), second), axis=1)[:, : 2 * HD]
        hidden = hidden + jnp.dot(
            both.astype(bf16), w_ref[p * 2 * HD : (p + 1) * 2 * HD, :], preferred_element_type=f32
        )
    hidden = hidden.astype(bf16).astype(f32)
    normed = layer_norm(hidden, gain_ref[...][None], shift_ref[...][None])
    out_ref[0] = jnp.where(slot_ref[:, 0:1] >= 0, normed, 0.0).astype(bf16)


def count_before(values):
    place = jnp.arange(values.shape[0])
    earlier = (place[:, None] > place[None, :]).astype(bf16)
    return jnp.dot(earlier, values.astype(bf16), preferred_element_type=f32).astype(jnp.int32)


def routes(mask_tokens, assignment, me_x, me_block):
    blocks, _ = where_tokens(mask_tokens)
    listed = mask_tokens >= 0
    hit = listed[:, :, None] & (blocks[:, :, None] == jnp.arange(BLOCKS)[None, None, :])
    count = jnp.sum(hit.astype(jnp.int32), axis=1)
    held = (count + 1 - me_x) // 2
    block_total = jnp.sum(held, axis=0)
    first = count_before(jnp.concatenate((block_total, jnp.zeros((8,), jnp.int32))))
    column = first[None, :BLOCKS] + count_before(held)
    column = column.reshape(OWNERS, GROUPS, 8) - (first[0:BLOCKS:8] // 128 * 128)[None, :, None]
    rank = jnp.arange(3)
    pick = jnp.where(
        rank < held.reshape(OWNERS, GROUPS, 8)[..., None], column[..., None] + rank, -1
    ).reshape(OWNERS, GROUPS * SLOTS)
    pick = jnp.take(pick, assignment, axis=0).reshape(OWNERS, GROUPS, SLOTS)
    pick = pick.transpose(1, 0, 2).reshape(GROUPS, OWNERS * SLOTS)

    lists = jnp.take(mask_tokens, assignment, axis=0)
    blocks, local = where_tokens(lists)
    here = (lists >= 0) & (blocks == me_block)
    entry = jnp.arange(CAP)
    earlier = (entry[:, None] < entry[None, :]).astype(bf16)
    order = jnp.dot(here.astype(bf16), earlier, preferred_element_type=f32).astype(jnp.int32)
    hit = here[:, :, None] & (order[:, :, None] == jnp.arange(8)[None, None, :])
    act_pick = jnp.sum(jnp.where(hit, local[:, :, None] + 1, 0), axis=1) - 1

    own = lax.dynamic_index_in_dim(lists, me_block, 0, keepdims=False)
    own_block, _ = where_tokens(own)
    same = (own_block[:, None] == own_block[None, :]) & (own >= 0)[:, None]
    order = jnp.sum((same & (entry[:, None] < entry[None, :])).astype(jnp.int32), axis=0)
    slot = jnp.where(own >= 0, order % 2 * PART + own_block * 3 + order // 2, -1)
    home = jnp.where(own >= 0, own_block * 8 + order, -1)
    wide = (CAP, 128)
    return (
        first,
        pick,
        act_pick,
        jnp.broadcast_to(slot[:, None], wide),
        jnp.broadcast_to(home[:, None], wide),
    )


def qkv_call(*arrays):
    return pl.pallas_call(
        qkv_kernel,
        in_specs=[pl.BlockSpec(memory_space=pltpu.SMEM)]
        + [vmem()] * 4
        + [pl.BlockSpec(memory_space=pltpu.HBM), vmem()],
        out_specs=vmem(),
        out_shape=jax.ShapeDtypeStruct((2 * HEADS, ROWS, 128), bf16),
        scratch_shapes=[
            pltpu.VMEM((D, 3 * D), bf16),
            pltpu.VMEM((2 * D, 128), f32),
            pltpu.VMEM((2 * D, 128), f32),
            pltpu.VMEM((2, D, 128), f32),
            pltpu.SemaphoreType.DMA((3,)),
        ],
        compiler_params=params(60),
        cost_estimate=pl.CostEstimate(flops=2 * TOK * D * 3 * D, bytes_accessed=14 * MIB, transcendentals=0),
        name="projection",
    )(*arrays)


def attend_call(*arrays):
    return pl.pallas_call(
        attend_kernel,
        in_specs=[pl.BlockSpec(memory_space=pltpu.SMEM), vmem(), vmem()],
        out_specs=vmem(),
        out_shape=jax.ShapeDtypeStruct((OWNERS, PART, 128), bf16),
        scratch_shapes=[
            pltpu.VMEM((TOKENS, 256), bf16),
            pltpu.VMEM((HP, TOKENS), bf16),
            pltpu.VMEM((HD, COLUMNS + 6 * 128), f32),
            pltpu.VMEM((256, BQ), bf16),
            pltpu.VMEM((HP, COLUMNS + WINDOW), f32),
            pltpu.VMEM((GROUPS, OWNERS * SLOTS, 128), f32),
        ],
        compiler_params=params(60),
        cost_estimate=pl.CostEstimate(
            flops=4 * COLUMNS * TOKENS * 256, bytes_accessed=8 * MIB, transcendentals=COLUMNS * TOKENS
        ),
        name="attend",
    )(*arrays)


def finish_call(*arrays):
    return pl.pallas_call(
        final_kernel,
        in_specs=[vmem()] * 8,
        out_specs=vmem(),
        out_shape=jax.ShapeDtypeStruct((1, CAP, D), bf16),
        scratch_shapes=[pltpu.VMEM((CAP, HEADS * 128), bf16)],
        compiler_params=params(30),
        cost_estimate=pl.CostEstimate(flops=2 * TOK * D * D, bytes_accessed=10 * MIB, transcendentals=0),
        name="finish",
    )(*arrays)


def local(
    activations,
    attn_gain,
    attn_shift,
    w_qkv,
    b_qkv,
    w_out,
    b_out,
    final_gain,
    final_shift,
    mask_tokens,
    assignment,
):
    tokens = activations.reshape(TOK, D)
    axes = ("tm", "y", "x")
    me_x = lax.axis_index("x")
    me_block = lax.axis_index("tm") * 8 + lax.axis_index("y") * 2 + me_x

    sent = qkv_call(me_block[None], tokens, attn_gain, attn_shift, mask_tokens, w_qkv, b_qkv)
    arrived = lax.all_to_all(sent, axes, 0, 0, tiled=True)

    first, pick, act_pick, slot, home = routes(mask_tokens, assignment, me_x, me_block)
    act_choose = (act_pick.reshape(OWNERS * 8, 1) == jnp.arange(TOK)[None, :]).astype(bf16)
    act_out = jnp.dot(act_choose, tokens, preferred_element_type=f32).astype(bf16)
    act_out, arrived = lax.optimization_barrier((act_out.reshape(OWNERS, 8, D), arrived))
    act_in = lax.all_to_all(act_out, axes, 0, 0, tiled=True)

    o_in = lax.all_to_all(attend_call(first, arrived, pick), axes, 0, 0, tiled=True)
    return finish_call(
        o_in, act_in.reshape(OWNERS * 8, D), slot, home, w_out, b_out, final_gain, final_shift
    )


def solution(mesh):
    times, spaces, clips = (mesh.shape[a] for a in ("tm", "space", "clip"))
    fine = Mesh(mesh.devices.reshape(times, spaces // 2, 2, clips), ("tm", "y", "x", "clip"))
    in_specs = (
        P(("clip", "tm"), ("y", "x"), None),
        P(),
        P(),
        P(),
        P(),
        P(),
        P(),
        P(),
        P(),
        P("clip", None),
        P("clip"),
    )
    out_specs = P(("clip", "tm", "y", "x"), None, None)
    return jax.shard_map(local, mesh=fine, in_specs=in_specs, out_specs=out_specs, check_vma=False)
```

time: 276 us -> 130 us (0.47)
  matrix products: 91.7 us -> 1.69 us
  local copies, waits for them, and re-layouts: 70.4 us -> 4.96 us
  Pallas kernels: 0 us -> 52.9 us
  other arithmetic: 24.7 us -> 1.86 us
  blocking collectives: 21.5 us -> 0 us
  between operations: 14 us -> 0.34 us
  waiting for transfers between devices: 32.5 us -> 44.1 us
    dot_general x34 -> x4, matrix products: 91.7 us -> 1.69 us  [the longest x1 1.27 us: local(): jnp.dot(act_choose, tokens, preferred_element_type=f32).astype(bf16)]
    pallas_call x0 -> x3, Pallas kernels: none -> 52.9 us  [the longest x1 41.1 us: attend_call(): pl.pallas_call(attend_kernel, in_specs=[pl.BlockSpec(memory_space=pltpu.S...]
    all_to_all x1 -> x0, blocking collectives: 21.5 us -> none  [items_in_groups(): lax.all_to_all(group, axis, split_axis=split_dim, concat_axis=concat_dim,...]
    while x48 -> x0, local copies, waits for them, and re-layouts: 20.2 us -> none
    slice x12 -> x1, local copies, waits for them, and re-layouts: 17.7 us -> 0.09 us  [routes(): first[0:BLOCKS:8] // 128 * 128]
    all_to_all x4 -> x3, waiting for transfers between devices: 27.9 us -> 44.1 us  [the longest x1 31.1 us: local(): arrived = lax.all_to_all(sent, axes, 0, 0, tiled=True)]
    reduce_sum x21 -> x4, other arithmetic: 16 us -> 1.41 us  [the longest x1 0.62 us: routes(): act_pick = jnp.sum(jnp.where(hit, local[:, :, None] + 1, 0), axis=1) - 1]
    another operation x8 -> x0, local copies, waits for them, and re-layouts: 13.5 us -> none  [the longest x4 12.7 us: local(): jnp.stack((query_rows, paired[0], paired[1]))]
  transfers between devices with their start and end apart: 6 -> 3, of which waited for: 4 -> 2; matrix products, arithmetic and copies ran while one was open for 42% -> 5% of each run, Pallas kernels for 0% -> 32%
where the time goes in v2:
time: 130 us; the launch traced here: 128 us
  Pallas kernels  52.9 us (41%)
  waiting for transfers between devices  44.1 us (34%)
  starting transfers between devices  21.9 us (17%)
  local copies, waits for them, and re-layouts  4.96 us (4%)
  other arithmetic  1.86 us (1%)
  matrix products  1.69 us (1%)
    pallas_call x1, Pallas kernels, attend_call(): pl.pallas_call(attend_kernel, in_specs=[pl.BlockSpec(memory_space=pltpu.S...  41.1 us
    all_to_all x1, waiting for transfers between devices, local(): arrived = lax.all_to_all(sent, axes, 0, 0, tiled=True)  31.1 us
    all_to_all x1, waiting for transfers between devices, local(): lax.all_to_all(attend_call(first, arrived, pick), axes, 0, 0, tiled=True)  13 us
    all_to_all x1, starting transfers between devices, local(): arrived = lax.all_to_all(sent, axes, 0, 0, tiled=True)  9.49 us
    pallas_call x1, Pallas kernels, qkv_call(): pl.pallas_call(qkv_kernel, in_specs=[pl.BlockSpec(memory_space=pltpu.SMEM...  8.68 us
    all_to_all x1, starting transfers between devices, local(): lax.all_to_all(attend_call(first, arrived, pick), axes, 0, 0, tiled=True)  7.38 us
    all_to_all x1, starting transfers between devices, local(): act_in = lax.all_to_all(act_out, axes, 0, 0, tiled=True)  5.04 us
    pallas_call x1, Pallas kernels, finish_call(): pl.pallas_call(final_kernel, in_specs=[vmem()] * 8, out_specs=vmem(), out...  3.09 us
  transfers between devices with their start and end apart: 3, of which 2 were waited for; matrix products, arithmetic and copies ran while one was open for 5% of the time, Pallas kernels for 32%

profile of v2, /device:TPU:0, one launch (start us, length us, event | category | flops | bytes accessed | tf_op | source)
XLA Modules:
  0.0 127.8 jit_solution(13423251281611316381)
XLA Ops:
  0.0 8.7 %projection.1 = bf16[32,336,128]{2,1,0:T(8,128)(2,1)} custom-call(s32[1]{0:T(128)} %bitcast.4.me_ref, bf16[192,1408]{1,0:T(8,128)(2,1)} %bitcast.41, f32[1408]{0:T(1024)} %gain_ref.2, f32[1408]{0:T(1024)} %shift_ref.2, s32[32,192]{1,0:T(8,128)} %lists_ref.1, bf16[1408,4224]{1,0:T(8,128)(2,1)} %w_ref.2, f32[4224]{0:T(1024)} %bias_ref.2), custom_call_target="tpu_custom_call" | custom-call | flops 2283798528 | bytes 14680064 | tf_op jit(solution)/shard_map/projection/pallas_call | solution.py:351
  8.7 9.5 %all-to-all-start = ((bf16[32,336,128]{2,1,0:T(8,128)(2,1)}), bf16[32,336,128]{2,1,0:T(8,128)(2,1)S(1)}, u32[]{:S(2)}, u32[]{:S(2)}) async-start(bf16[32,336,128]{2,1,0:T(8,128)(2,1)} %projection.1), calls=%async_computation | async-start | bytes 5505024 | tf_op jit(solution)/shard_map/all_to_all | solution.py:425
  18.3 0.6 convert_reduce_fusion
  19.0 0.6 gather_fusion
  19.6 0.1 fusion.7
  19.7 0.1 convolution_convert_fusion.1
  19.9 0.6 select_reduce_fusion
  20.6 0.1 fusion.2.first_ref
  20.7 0.1 slice.7
  20.9 0.1 fusion.1
  21.5 0.1 lt.80
  21.6 0.6 gather_fusion.1
  22.2 0.1 gather.12
  22.3 0.1 select_bitcast_fusion
  22.4 0.7 reshape.206.pick_ref
  23.1 1.3 fusion
  24.4 31.1 %all-to-all-done.in_ref = bf16[32,336,128]{2,1,0:T(8,128)(2,1)S(1)} async-done(((bf16[32,336,128]{2,1,0:T(8,128)(2,1)}), bf16[32,336,128]{2,1,0:T(8,128)(2,1)S(1)}, u32[]{:S(2)}, u32[]{:S(2)}) %all-to-all-start) | async-done | bytes 2752544 | tf_op jit(solution)/shard_map/all_to_all | solution.py:425
  55.6 5.0 %all-to-all-start.2 = ((bf16[32,8,1408]{2,1,0:T(8,128)(2,1)}), bf16[32,8,1408]{2,1,0:T(8,128)(2,1)S(1)}, u32[]{:S(2)}, u32[]{:S(2)}) async-start(bf16[32,8,1408]{2,1,0:T(8,128)(2,1)} %fusion), calls=%async_computation.2 | async-start | bytes 1441792 | tf_op jit(solution)/shard_map/all_to_all | solution.py:431
  60.7 41.1 %attend.1 = bf16[32,96,128]{2,1,0:T(8,128)(2,1)} custom-call(s32[40]{0:T(128)} %copy-done.8, bf16[32,336,128]{2,1,0:T(8,128)(2,1)} %copy-done.5, s32[4,768]{1,0:T(4,128)} %reshape.206.pick_ref), custom_call_target="tpu_custom_call" | custom-call | flops 19327352832 | bytes 8388608 | tf_op jit(solution)/shard_map/attend/pallas_call | solution.py:372
  101.8 7.4 %all-to-all-start.1 = ((bf16[32,96,128]{2,1,0:T(8,128)(2,1)}), bf16[32,96,128]{2,1,0:T(8,128)(2,1)S(1)}, u32[]{:S(2)}, u32[]{:S(2)}) async-start(bf16[32,96,128]{2,1,0:T(8,128)(2,1)} %attend.1), calls=%async_computation.1 | async-start | bytes 1572864 | tf_op jit(solution)/shard_map/all_to_all | solution.py:433
  109.2 0.1 convert_reduce_fusion.1
  109.4 13.0 %all-to-all-done.1.o_ref = bf16[32,96,128]{2,1,0:T(8,128)(2,1)S(1)} async-done(((bf16[32,96,128]{2,1,0:T(8,128)(2,1)}), bf16[32,96,128]{2,1,0:T(8,128)(2,1)S(1)}, u32[]{:S(2)}, u32[]{:S(2)}) %all-to-all-start.1) | async-done | bytes 786464 | tf_op jit(solution)/shard_map/all_to_all | solution.py:433
  122.6 2.1 %copy-done = bf16[1408,1408]{1,0:T(8,128)(2,1)S(1)} copy-done((bf16[1408,1408]{1,0:T(8,128)(2,1)S(1)}, bf16[1408,1408]{1,0:T(8,128)(2,1)}, u32[]{:S(2)}) %copy-start) | copy-done | bytes 3964952
  124.7 3.1 %finish.1 = bf16[1,192,1408]{2,1,0:T(8,128)(2,1)} custom-call(bf16[32,96,128]{2,1,0:T(8,128)(2,1)S(1)} %all-to-all-done.1.o_ref, bf16[256,1408]{1,0:T(8,128)(2,1)S(1)} %bitcast.40, s32[192,128]{1,0:T(8,128)S(1)} %broadcast_in_dim.56.slot_ref, s32[192,128]{1,0:T(8,128)S(1)} %broadcast_in_dim.90.home_ref, bf16[1408,1408]{1,0:T(8,128)(2,1)S(1)} %copy-done, ...), custom_call_target="tpu_custom_call" | custom-call | flops 761266176 | bytes 10485760 | tf_op jit(solution)/shard_map/finish/pallas_call | solution.py:394
  (48 shorter events, 1.0 us)
Async XLA Ops:
  8.7 9.5 %copy-start.4 = (s32[32,192]{1,0:T(8,128)S(1)}, s32[32,192]{1,0:T(8,128)}, u32[]{:S(2)}) copy-start(s32[32,192]{1,0:T(8,128)} %lists_ref.1) | copy-start | bytes 73732
  8.7 10.2 %copy-start.7 = (s32[32]{0:T(128)S(1)}, s32[32]{0:T(128)}, u32[]{:S(2)}) copy-start(s32[32]{0:T(128)} %param.21) | copy-start | bytes 388
  8.7 14.4 %copy-start.6 = (bf16[6,32,1408]{2,1,0:T(8,128)(2,1)S(1)}, bf16[6,32,1408]{2,1,0:T(8,128)(2,1)}, u32[]{:S(2)}) copy-start(bf16[6,32,1408]{2,1,0:T(8,128)(2,1)} %param.11) | copy-start | bytes 1622020
  8.7 46.8 %all-to-all-start = ((bf16[32,336,128]{2,1,0:T(8,128)(2,1)}), bf16[32,336,128]{2,1,0:T(8,128)(2,1)S(1)}, u32[]{:S(2)}, u32[]{:S(2)}) async-start(bf16[32,336,128]{2,1,0:T(8,128)(2,1)} %projection.1), calls=%async_computation | async-start | bytes 5505024 | tf_op jit(solution)/shard_map/all_to_all | solution.py:425
  20.7 39.9 %copy-start.8 = (s32[40]{0:T(128)}, s32[40]{0:T(128)S(1)}, u32[]{:S(2)}) copy-start(s32[40]{0:T(128)S(1)} %fusion.2.first_ref) | copy-start | bytes 484
  55.5 5.1 %copy-start.5 = (bf16[32,336,128]{2,1,0:T(8,128)(2,1)}, bf16[32,336,128]{2,1,0:T(8,128)(2,1)S(1)}, u32[]{:S(2)}) copy-start(bf16[32,336,128]{2,1,0:T(8,128)(2,1)S(1)} %all-to-all-done.in_ref) | copy-start | bytes 8257540
  55.6 46.2 %all-to-all-start.2 = ((bf16[32,8,1408]{2,1,0:T(8,128)(2,1)}), bf16[32,8,1408]{2,1,0:T(8,128)(2,1)S(1)}, u32[]{:S(2)}, u32[]{:S(2)}) async-start(bf16[32,8,1408]{2,1,0:T(8,128)(2,1)} %fusion), calls=%async_computation.2 | async-start | bytes 1441792 | tf_op jit(solution)/shard_map/all_to_all | solution.py:431
  60.6 61.9 %copy-start.1 = (f32[1408]{0:T(1024)S(1)}, f32[1408]{0:T(1024)}, u32[]{:S(2)}) copy-start(f32[1408]{0:T(1024)} %bias_ref.3) | copy-start | bytes 16900
  60.6 61.9 %copy-start.2 = (f32[1408]{0:T(1024)S(1)}, f32[1408]{0:T(1024)}, u32[]{:S(2)}) copy-start(f32[1408]{0:T(1024)} %gain_ref.3) | copy-start | bytes 16900
  60.6 61.9 %copy-start.3 = (f32[1408]{0:T(1024)S(1)}, f32[1408]{0:T(1024)}, u32[]{:S(2)}) copy-start(f32[1408]{0:T(1024)} %shift_ref.3) | copy-start | bytes 16900
  101.8 20.6 %all-to-all-start.1 = ((bf16[32,96,128]{2,1,0:T(8,128)(2,1)}), bf16[32,96,128]{2,1,0:T(8,128)(2,1)S(1)}, u32[]{:S(2)}, u32[]{:S(2)}) async-start(bf16[32,96,128]{2,1,0:T(8,128)(2,1)} %attend.1), calls=%async_computation.1 | async-start | bytes 1572864 | tf_op jit(solution)/shard_map/all_to_all | solution.py:433
  122.6 2.1 %copy-start = (bf16[1408,1408]{1,0:T(8,128)(2,1)S(1)}, bf16[1408,1408]{1,0:T(8,128)(2,1)}, u32[]{:S(2)}) copy-start(bf16[1408,1408]{1,0:T(8,128)(2,1)} %w_ref.3) | copy-start | bytes 11894788

commit v3 on v2

--- a/solution.py
+++ b/solution.py
@@ -26,6 +26,7 @@
 QROWS = 72
 ROWS = 3 * HD + QROWS
 GROUPS = 4
+PACK = 2 * QROWS
 SLOTS = 24
 WINDOW = 8 * PART + 128
 BQ = 512
@@ -80,13 +81,14 @@
         lax.broadcasted_iota(jnp.int32, (OWNERS, OWNERS), 0)
         > lax.broadcasted_iota(jnp.int32, (OWNERS, OWNERS), 1)
     ).astype(bf16)
-    bases = []
-    for part in range(2):
-        held = jnp.zeros_like(count)
-        for k in range(part, EACH, 2):
-            held = held + ones_where(count > k)
+    odd = ((lax.broadcasted_iota(jnp.int32, (OWNERS, 1), 0) + me) & 1) == 1
+    bases, many, few = [], jnp.zeros_like(count), jnp.zeros_like(count)
+    for k in range(0, EACH, 2):
+        many, few = many + ones_where(count > k), few + ones_where(count > k + 1)
+    for held in (jnp.where(odd, few, many), jnp.where(odd, many, few)):
         held = jnp.broadcast_to(held, (OWNERS, 128)).astype(bf16)
-        bases.append(jnp.dot(lower, held, preferred_element_type=f32)[:, 0:1] + part * PART)
+        bases.append(jnp.dot(lower, held, preferred_element_type=f32)[:, 0:1] + len(bases) * PART)
+    bases = (jnp.where(odd, bases[1], bases[0]), jnp.where(odd, bases[0], bases[1]))
     lane = lax.broadcasted_iota(jnp.int32, (OWNERS, CAP), 1).astype(f32)
     slots, tokens = [], []
     for k in range(EACH):
@@ -218,7 +220,7 @@
     acc[:, at] = total / total[HD : HD + 1, :]
 
 
-def attend_kernel(first_ref, in_ref, pick_ref, out_ref, keys, values, columns, queries, acc, rows):
+def attend_kernel(first_ref, in_ref, pick_ref, act_ref, out_ref, keys, values, columns, queries, acc, rows):
     columns[:, 0:128] = jnp.zeros((HD, 128), f32)
 
     def pair(p, largest):
@@ -267,24 +269,51 @@
 
     def owner(d, carried):
         at = pl.ds(pl.multiple_of(d * SLOTS, 8), SLOTS)
-        out_ref[d] = jnp.concatenate([rows[g, at, :] for g in range(GROUPS)], axis=0).astype(bf16)
+        found = jnp.concatenate([rows[g, at, :] for g in range(GROUPS - 1)], axis=0)
+        last = rows[GROUPS - 1, at, :]
+        spread = jnp.concatenate([pltpu.roll(last, HD - 40 * i, 1) for i in range(3)], axis=0)
+        packed = jnp.where(lanes_below((QROWS, 128), HD), found, spread)
+        out_ref[d] = jnp.concatenate((packed, act_ref[d].astype(f32)), axis=0).astype(bf16)
         return carried
 
     lax.fori_loop(0, OWNERS, owner, 0)
 
 
 def final_kernel(
-    o_ref, act_ref, slot_ref, home_ref, w_ref, bias_ref, gain_ref, shift_ref, out_ref, attended
+    in_ref, slot_ref, home_ref, w_ref, bias_ref, gain_ref, shift_ref, out_ref, attended, acts
 ):
+    shape = (SLOTS, 128)
     for h in range(HEADS):
         for x in range(2):
-            attended[x * 96 : x * 96 + 96, h * 128 : h * 128 + 128] = o_ref[2 * h + x]
+            whole = in_ref[2 * h + x].astype(f32)
+            parts = [pltpu.roll(whole[SLOTS * i : SLOTS * i + SLOTS], 40 * (i + 1), 1) for i in range(3)]
+            last = jnp.where(
+                lanes_below(shape, 40), parts[0], jnp.where(lanes_below(shape, 80), parts[1], parts[2])
+            )
+            attended[x * PART : x * PART + PART, h * 128 : h * 128 + 128] = jnp.concatenate(
+                (whole[:QROWS], last), axis=0
+            ).astype(bf16)
+            at = 8 * (2 * h + x)
+            for c in range(9):
+                acts[at : at + 8, c * 128 : c * 128 + 128] = whole[QROWS + 8 * c : QROWS + 8 * c + 8]
     slot = lax.broadcasted_iota(jnp.int32, (CAP, CAP), 1)
-    choose = jnp.where(slot == slot_ref[:, 0:1], 1.0, 0.0).astype(bf16)
+    choose = ones_where(slot == slot_ref[:, 0:1]).astype(bf16)
     listed_rows = jnp.dot(choose, attended[...], preferred_element_type=f32)
-    place = lax.broadcasted_iota(jnp.int32, (CAP, OWNERS * 8), 1)
-    choose = jnp.where(place == home_ref[:, 0:1], 1.0, 0.0).astype(bf16)
-    tokens = jnp.dot(choose, act_ref[...], preferred_element_type=f32)
+    place = lax.broadcasted_iota(jnp.int32, (CAP, BLOCKS * 8), 1)
+    home = home_ref[:, 0:1]
+    choose = ones_where(place == home).astype(bf16)
+    got = acts[...].astype(bf16)
+    tokens = jnp.dot(choose, got, preferred_element_type=f32)
+    tail = jnp.zeros((CAP, 256), f32)
+    rank = home & 7
+    for i in range(3):
+        there = jnp.where((home >= 0) & (rank >> 1 == i), home - rank + EACH + (rank & 1), -1)
+        choose = ones_where(place == there).astype(bf16)
+        pair = jnp.concatenate(
+            (got[:, i * 128 : i * 128 + 128], got[:, (i + 3) * 128 : (i + 4) * 128]), axis=1
+        )
+        tail = tail + jnp.dot(choose, pair, preferred_element_type=f32)
+    tokens = jnp.concatenate((tokens, tail), axis=1)
     hidden = tokens + bias_ref[...][None]
     low = lanes_below((CAP, 128), HD)
     for p in range(HEADS // 2):
@@ -310,7 +339,8 @@
     listed = mask_tokens >= 0
     hit = listed[:, :, None] & (blocks[:, :, None] == jnp.arange(BLOCKS)[None, None, :])
     count = jnp.sum(hit.astype(jnp.int32), axis=1)
-    held = (count + 1 - me_x) // 2
+    odd = (jnp.arange(OWNERS)[:, None] + jnp.arange(BLOCKS)[None, :]) % 2
+    held = (count + (odd == me_x)) // 2
     block_total = jnp.sum(held, axis=0)
     first = count_before(jnp.concatenate((block_total, jnp.zeros((8,), jnp.int32))))
     column = first[None, :BLOCKS] + count_before(held)
@@ -335,7 +365,8 @@
     own_block, _ = where_tokens(own)
     same = (own_block[:, None] == own_block[None, :]) & (own >= 0)[:, None]
     order = jnp.sum((same & (entry[:, None] < entry[None, :])).astype(jnp.int32), axis=0)
-    slot = jnp.where(own >= 0, order % 2 * PART + own_block * 3 + order // 2, -1)
+    half = (order + own_block + lax.dynamic_index_in_dim(assignment, me_block, 0, keepdims=False)) % 2
+    slot = jnp.where(own >= 0, half * PART + own_block * 3 + order // 2, -1)
     home = jnp.where(own >= 0, own_block * 8 + order, -1)
     wide = (CAP, 128)
     return (
@@ -345,6 +376,15 @@
         jnp.broadcast_to(slot[:, None], wide),
         jnp.broadcast_to(home[:, None], wide),
     )
+
+
+def pack_rows(act_pick, tokens):
+    choose = (act_pick[:, :EACH].reshape(OWNERS * EACH, 1) == jnp.arange(TOK)[None, :]).astype(bf16)
+    found = jnp.dot(choose, tokens, preferred_element_type=f32).astype(bf16)
+    tiles = found.reshape(OWNERS, EACH, 11, 128).transpose(0, 2, 1, 3)
+    last = tiles[:, 9:].reshape(OWNERS, EACH, 2, 128)
+    last = jnp.concatenate((last, jnp.zeros((OWNERS, 3, 2, 128), bf16)), axis=1)
+    return jnp.concatenate((tiles[:, :9], last), axis=2).reshape(OWNERS, QROWS, 128)
 
 
 def qkv_call(*arrays):
@@ -371,9 +411,9 @@
 def attend_call(*arrays):
     return pl.pallas_call(
         attend_kernel,
-        in_specs=[pl.BlockSpec(memory_space=pltpu.SMEM), vmem(), vmem()],
+        in_specs=[pl.BlockSpec(memory_space=pltpu.SMEM), vmem(), vmem(), vmem()],
         out_specs=vmem(),
-        out_shape=jax.ShapeDtypeStruct((OWNERS, PART, 128), bf16),
+        out_shape=jax.ShapeDtypeStruct((OWNERS, PACK, 128), bf16),
         scratch_shapes=[
             pltpu.VMEM((TOKENS, 256), bf16),
             pltpu.VMEM((HP, TOKENS), bf16),
@@ -382,7 +422,7 @@
             pltpu.VMEM((HP, COLUMNS + WINDOW), f32),
             pltpu.VMEM((GROUPS, OWNERS * SLOTS, 128), f32),
         ],
-        compiler_params=params(60),
+        compiler_params=params(30),
         cost_estimate=pl.CostEstimate(
             flops=4 * COLUMNS * TOKENS * 256, bytes_accessed=8 * MIB, transcendentals=COLUMNS * TOKENS
         ),
@@ -393,10 +433,10 @@
 def finish_call(*arrays):
     return pl.pallas_call(
         final_kernel,
-        in_specs=[vmem()] * 8,
+        in_specs=[vmem()] * 7,
         out_specs=vmem(),
         out_shape=jax.ShapeDtypeStruct((1, CAP, D), bf16),
-        scratch_shapes=[pltpu.VMEM((CAP, HEADS * 128), bf16)],
+        scratch_shapes=[pltpu.VMEM((CAP, HEADS * 128), bf16), pltpu.VMEM((BLOCKS * 8, 9 * 128), f32)],
         compiler_params=params(30),
         cost_estimate=pl.CostEstimate(flops=2 * TOK * D * D, bytes_accessed=10 * MIB, transcendentals=0),
         name="finish",
@@ -425,15 +465,10 @@
     arrived = lax.all_to_all(sent, axes, 0, 0, tiled=True)
 
     first, pick, act_pick, slot, home = routes(mask_tokens, assignment, me_x, me_block)
-    act_choose = (act_pick.reshape(OWNERS * 8, 1) == jnp.arange(TOK)[None, :]).astype(bf16)
-    act_out = jnp.dot(act_choose, tokens, preferred_element_type=f32).astype(bf16)
-    act_out, arrived = lax.optimization_barrier((act_out.reshape(OWNERS, 8, D), arrived))
-    act_in = lax.all_to_all(act_out, axes, 0, 0, tiled=True)
-
-    o_in = lax.all_to_all(attend_call(first, arrived, pick), axes, 0, 0, tiled=True)
-    return finish_call(
-        o_in, act_in.reshape(OWNERS * 8, D), slot, home, w_out, b_out, final_gain, final_shift
-    )
+    act_out = pack_rows(act_pick, tokens)
+    first, pick, act_out, slot, home = lax.optimization_barrier((first, pick, act_out, slot, home))
+    o_in = lax.all_to_all(attend_call(first, arrived, pick, act_out), axes, 0, 0, tiled=True)
+    return finish_call(o_in, slot, home, w_out, b_out, final_gain, final_shift)
 
 
 def solution(mesh):

time: 130 us -> 123 us (0.946); the launches traced: 128 us -> 123 us
  blocking collectives: 0 us -> 29.7 us
  waiting for transfers between devices: 44.1 us -> 26.5 us
  starting transfers between devices: 21.9 us -> 9.36 us
  Pallas kernels: 52.9 us -> 46.4 us
  other arithmetic: 1.86 us -> 4.31 us
    all_to_all x0 -> x1, blocking collectives: none -> 29.7 us  [local(): lax.all_to_all(attend_call(first, arrived, pick, act_out), axes, 0, 0, ti...]
    all_to_all x2 -> x0, waiting for transfers between devices: 13 us -> none  [the longest x1 13 us: local(): lax.all_to_all(attend_call(first, arrived, pick), axes, 0, 0, tiled=True)]
    all_to_all x2 -> x0, starting transfers between devices: 12.4 us -> none  [the longest x1 7.38 us: local(): lax.all_to_all(attend_call(first, arrived, pick), axes, 0, 0, tiled=True)]
    pallas_call x1, Pallas kernels: 41.1 us -> 34.5 us  [attend_call(): pl.pallas_call(attend_kernel, in_specs=[pl.BlockSpec(memory_space=pltpu.S...]
    all_to_all x1, waiting for transfers between devices: 31.1 us -> 26.5 us  [local(): arrived = lax.all_to_all(sent, axes, 0, 0, tiled=True)]
    unnamed x19 -> x17, local copies, waits for them, and re-layouts: 2.17 us -> 0.05 us
    reshape x0 -> x2, local copies, waits for them, and re-layouts: none -> 1.49 us  [the longest x1 1.42 us: pack_rows(): tiles = found.reshape(OWNERS, EACH, 11, 128).transpose(0, 2, 1, 3)]
  transfers between devices with their start and end apart: 3 -> 1, of which waited for: 2 -> 1; matrix products, arithmetic and copies ran while one was open for 5% -> 9% of each run, Pallas kernels for 32% -> 0%
where the time goes in v3:
time: 123 us
  Pallas kernels  46.4 us (38%)
  blocking collectives  29.7 us (24%)
  waiting for transfers between devices  26.5 us (22%)
  starting transfers between devices  9.36 us (8%)
  local copies, waits for them, and re-layouts  4.71 us (4%)
  other arithmetic  4.31 us (4%)
  matrix products  1.57 us (1%)
    pallas_call x1, Pallas kernels, attend_call(): pl.pallas_call(attend_kernel, in_specs=[pl.BlockSpec(memory_space=pltpu.S...  34.5 us
    all_to_all x1, blocking collectives, local(): lax.all_to_all(attend_call(first, arrived, pick, act_out), axes, 0, 0, ti...  29.7 us
    all_to_all x1, waiting for transfers between devices, local(): arrived = lax.all_to_all(sent, axes, 0, 0, tiled=True)  26.5 us
    all_to_all x1, starting transfers between devices, local(): arrived = lax.all_to_all(sent, axes, 0, 0, tiled=True)  9.36 us
    pallas_call x1, Pallas kernels, qkv_call(): pl.pallas_call(qkv_kernel, in_specs=[pl.BlockSpec(memory_space=pltpu.SMEM...  8.68 us
    pallas_call x1, Pallas kernels, finish_call(): pl.pallas_call(final_kernel, in_specs=[vmem()] * 7, out_specs=vmem(), out...  3.23 us
  transfers between devices with their start and end apart: 1, of which 1 were waited for; matrix products, arithmetic and copies ran while one was open for 9% of the time, Pallas kernels for 0%

profile of v3, /device:TPU:0, one launch (start us, length us, event | category | flops | bytes accessed | tf_op | source)
XLA Modules:
  0.0 122.8 jit_solution(10319499783301687134)
XLA Ops:
  0.0 8.7 %projection.1 = bf16[32,336,128]{2,1,0:T(8,128)(2,1)} custom-call(s32[1]{0:T(128)} %bitcast.11.me_ref, bf16[192,1408]{1,0:T(8,128)(2,1)} %bitcast.36, f32[1408]{0:T(1024)} %gain_ref.2, f32[1408]{0:T(1024)} %shift_ref.2, s32[32,192]{1,0:T(8,128)} %lists_ref.1, bf16[1408,4224]{1,0:T(8,128)(2,1)} %w_ref.2, f32[4224]{0:T(1024)} %bias_ref.2), custom_call_target="tpu_custom_call" | custom-call | flops 2283798528 | bytes 14680064 | tf_op jit(solution)/shard_map/projection/pallas_call | solution.py:391
  8.7 9.4 %all-to-all-start = ((bf16[32,336,128]{2,1,0:T(8,128)(2,1)}), bf16[32,336,128]{2,1,0:T(8,128)(2,1)S(1)}, u32[]{:S(2)}, u32[]{:S(2)}) async-start(bf16[32,336,128]{2,1,0:T(8,128)(2,1)} %projection.1), calls=%async_computation | async-start | bytes 5505024 | tf_op jit(solution)/shard_map/all_to_all | solution.py:465
  18.2 0.6 gather_fusion.1
  18.9 0.1 convolution_convert_fusion.1
  19.1 0.6 select_reduce_fusion
  19.7 0.6 convert_reduce_fusion
  20.4 0.7 dynamic_slice.9
  21.4 0.1 fusion.2.first_ref
  21.6 0.1 fusion.1
  22.0 0.1 add_select_fusion
  22.3 0.6 gather_fusion
  23.2 1.2 convolution_convert_fusion
  24.3 1.4 %reshape.230 = bf16[32,6,11,128]{3,2,1,0:T(8,128)(2,1)S(1)} reshape(bf16[192,1408]{1,0:T(8,128)(2,1)} %convolution_convert_fusion) | data formatting | bytes 1081344 | tf_op jit(solution)/shard_map/reshape | solution.py:384
  25.8 0.1 slice.26
  26.0 0.3 fusion.3
  26.3 0.2 copy.30
  26.4 0.7 compare_reduce_fusion
  27.2 0.7 multiply_add_fusion.1
  27.9 0.1 convert_reduce_fusion.1
  28.0 0.7 add_select_fusion.5
  28.9 26.5 %all-to-all-done.in_ref = bf16[32,336,128]{2,1,0:T(8,128)(2,1)S(1)} async-done(((bf16[32,336,128]{2,1,0:T(8,128)(2,1)}), bf16[32,336,128]{2,1,0:T(8,128)(2,1)S(1)}, u32[]{:S(2)}, u32[]{:S(2)}) %all-to-all-start) | async-done | bytes 2752544 | tf_op jit(solution)/shard_map/all_to_all | solution.py:465
  55.4 34.5 %attend.1 = bf16[32,144,128]{2,1,0:T(8,128)(2,1)S(1)} custom-call(s32[40]{0:T(128)S(1)} %fusion.2.first_ref, bf16[32,336,128]{2,1,0:T(8,128)(2,1)S(1)} %all-to-all-done.in_ref, s32[4,768]{1,0:T(4,128)S(1)} %reshape.228.pick_ref, bf16[32,72,128]{2,1,0:T(8,128)(2,1)S(1)} %bitcast.32), custom_call_target="tpu_custom_call" | custom-call | flops 19327352832 | bytes 8388608 | tf_op jit(solution)/shard_map/attend/pallas_call | solution.py:412
  89.9 29.7 %all_to_all.10.in_ref = bf16[32,144,128]{2,1,0:T(8,128)(2,1)S(1)} all-to-all(bf16[32,144,128]{2,1,0:T(8,128)(2,1)S(1)} %attend.1), channel_id=1, replica_groups=mesh['tm'=4,'y'=4,'x'=2,'clip'=4] {'tm','y','x'}, dimensions={0} | all-to-all | bytes 2359296 | tf_op jit(solution)/shard_map/all_to_all | solution.py:470
  119.6 3.2 %finish.1 = bf16[1,192,1408]{2,1,0:T(8,128)(2,1)} custom-call(bf16[32,144,128]{2,1,0:T(8,128)(2,1)S(1)} %all_to_all.10.in_ref, s32[192,128]{1,0:T(8,128)S(1)} %broadcast_in_dim.55.slot_ref, s32[192,128]{1,0:T(8,128)S(1)} %broadcast_in_dim.56.home_ref, bf16[1408,1408]{1,0:T(8,128)(2,1)S(1)} %copy-done, f32[1408]{0:T(1024)S(1)} %copy-done.1, ...), custom_call_target="tpu_custom_call" | custom-call | flops 761266176 | bytes 10485760 | tf_op jit(solution)/shard_map/finish/pallas_call | solution.py:434
  (51 shorter events, 1.6 us)
Async XLA Ops:
  8.7 9.4 %copy-start.7 = (s32[32]{0:T(128)S(1)}, s32[32]{0:T(128)}, u32[]{:S(2)}) copy-start(s32[32]{0:T(128)} %param.21) | copy-start | bytes 388
  8.7 9.4 %copy-start.4 = (s32[32,192]{1,0:T(8,128)S(1)}, s32[32,192]{1,0:T(8,128)}, u32[]{:S(2)}) copy-start(s32[32,192]{1,0:T(8,128)} %lists_ref.1) | copy-start | bytes 73732
  8.7 46.7 %all-to-all-start = ((bf16[32,336,128]{2,1,0:T(8,128)(2,1)}), bf16[32,336,128]{2,1,0:T(8,128)(2,1)S(1)}, u32[]{:S(2)}, u32[]{:S(2)}) async-start(bf16[32,336,128]{2,1,0:T(8,128)(2,1)} %projection.1), calls=%async_computation | async-start | bytes 5505024 | tf_op jit(solution)/shard_map/all_to_all | solution.py:465
  18.1 5.1 %copy-start.5 = (bf16[6,32,1408]{2,1,0:T(8,128)(2,1)S(1)}, bf16[6,32,1408]{2,1,0:T(8,128)(2,1)}, u32[]{:S(2)}) copy-start(bf16[6,32,1408]{2,1,0:T(8,128)(2,1)} %param.11) | copy-start | bytes 1622020
  18.9 0.9 copy-start.6
  55.4 64.2 %copy-start = (bf16[1408,1408]{1,0:T(8,128)(2,1)S(1)}, bf16[1408,1408]{1,0:T(8,128)(2,1)}, u32[]{:S(2)}) copy-start(bf16[1408,1408]{1,0:T(8,128)(2,1)} %w_ref.3) | copy-start | bytes 11894788
  89.9 29.7 %copy-start.1 = (f32[1408]{0:T(1024)S(1)}, f32[1408]{0:T(1024)}, u32[]{:S(2)}) copy-start(f32[1408]{0:T(1024)} %bias_ref.3) | copy-start | bytes 16900
  89.9 29.7 %copy-start.2 = (f32[1408]{0:T(1024)S(1)}, f32[1408]{0:T(1024)}, u32[]{:S(2)}) copy-start(f32[1408]{0:T(1024)} %gain_ref.3) | copy-start | bytes 16900
  89.9 29.7 %copy-start.3 = (f32[1408]{0:T(1024)S(1)}, f32[1408]{0:T(1024)}, u32[]{:S(2)}) copy-start(f32[1408]{0:T(1024)} %shift_ref.3) | copy-start | bytes 16900

commit v4 on v3

--- a/solution.py
+++ b/solution.py
@@ -153,7 +153,7 @@
 
 
 def put_keys(tile, k_tile, v_tile, keys, values):
-    at = pl.ds(pl.multiple_of(tile * 128, 128), 128)
+    at = pl.ds(tile * 128, 128)
     ones = jnp.ones((HP - HD, 128), f32)
     turned = jnp.concatenate((k_tile, ones, jnp.zeros((128 - HP, 128), f32)), axis=0).T.astype(bf16)
     keys[at, 0:128] = turned
@@ -192,19 +192,34 @@
     return jnp.dot(keys[pl.ds(first, count), :], queries[:, at], preferred_element_type=f32)
 
 
-def attend_columns(start, width, columns, queries, keys, values, acc, largest_key):
-    at = pl.ds(pl.multiple_of(start, 256), width)
+def start_columns(at, columns, queries, keys):
     scaled = columns[:, at] * QK_SCALE
     high = scaled.astype(bf16).astype(f32)
+    width = scaled.shape[1]
     zeros = jnp.zeros((128 - HD, width), f32)
     here = pl.ds(0, width)
     queries[0:128, here] = jnp.concatenate((high, zeros), axis=0).astype(bf16)
     queries[128:256, here] = jnp.concatenate((scaled - high, zeros), axis=0).astype(bf16)
     shift = jnp.max(scores_of(keys, queries, 0, 128, here), axis=0, keepdims=True)
     set_shift(queries, here, shift)
-    norm = jnp.sqrt(jnp.sum(scaled * scaled, axis=0, keepdims=True) * largest_key)
-
-    @pl.when(jnp.logical_not(jnp.max(norm * 1.01 - shift) <= SAFE))
+    return shift, jnp.sum(scaled * scaled, axis=0, keepdims=True)
+
+
+def unsafe(shift, square, largest_key):
+    return jnp.logical_not(jnp.max(jnp.sqrt(square * largest_key) * 1.01 - shift) <= SAFE)
+
+
+def weigh(keys, queries, values, first, width):
+    weights = jnp.exp2(scores_of(keys, queries, first, BK, pl.ds(0, width))).astype(bf16)
+    return jnp.dot(values[:, first : first + BK], weights, preferred_element_type=f32)
+
+
+def attend_columns(start, width, columns, queries, keys, values, acc, largest_key):
+    at = pl.ds(pl.multiple_of(start, 256), width)
+    here = pl.ds(0, width)
+    shift, square = start_columns(at, columns, queries, keys)
+
+    @pl.when(unsafe(shift, square, largest_key))
     def _():
         def step(i, above):
             got = scores_of(keys, queries, pl.multiple_of(i * 256, 256), 256, here)
@@ -213,32 +228,39 @@
         above = lax.fori_loop(0, TOKENS // 256, step, jnp.zeros((1, width), f32))
         set_shift(queries, here, shift + above)
 
-    total = jnp.zeros((HP, width), f32)
-    for first in range(0, TOKENS, BK):
-        weights = jnp.exp2(scores_of(keys, queries, first, BK, here)).astype(bf16)
-        total = total + jnp.dot(values[:, first : first + BK], weights, preferred_element_type=f32)
+    total = weigh(keys, queries, values, 0, width)
+    for first in range(BK, TOKENS, BK):
+        total = total + weigh(keys, queries, values, first, width)
     acc[:, at] = total / total[HD : HD + 1, :]
 
 
-def attend_kernel(first_ref, in_ref, pick_ref, act_ref, out_ref, keys, values, columns, queries, acc, rows):
+def unpack_keys(chunk, in_ref, keys, values):
+    largest = jnp.zeros((1, 128), f32)
+    for i in range(BLOCKS // 2):
+        if chunk < 2:
+            block = chunk * (BLOCKS // 2) + i
+            k_tile = in_ref[block, 0:96].astype(f32)[:HD]
+            v_tile = in_ref[block, 80:176].astype(f32)[8:]
+        else:
+            rests = [in_ref[2 * i + j, 176:272].astype(f32)[:HD] for j in range(2)]
+            k_tile, v_tile = unpack_pair(*rests)
+        square = put_keys(chunk * (BLOCKS // 2) + i, k_tile, v_tile, keys, values)
+        largest = jnp.maximum(largest, square)
+    return largest
+
+
+def attend_kernel(
+    first_ref, in_ref, pick_ref, act_ref, out_ref, keys, values, columns, queries, acc, rows
+):
     columns[:, 0:128] = jnp.zeros((HD, 128), f32)
 
-    def pair(p, largest):
-        rests = []
-        for j in range(2):
-            block = 2 * p + j
-            whole = in_ref[block].astype(f32)
-            square = put_keys(block, whole[0:HD], whole[HD : 2 * HD], keys, values)
-            largest = jnp.maximum(largest, square)
-            rests.append(whole[2 * HD : 3 * HD])
-            first = first_ref[block]
-            put_queries(whole[3 * HD :], first, first_ref[block + 1] - first, columns)
-        square = put_keys(BLOCKS + p, *unpack_pair(*rests), keys, values)
-        return jnp.maximum(largest, square)
-
-    largest = lax.fori_loop(0, BLOCKS // 2, pair, jnp.zeros((1, 128), f32))
-    largest_key = jnp.max(largest, axis=1, keepdims=True)
-
+    def place(block, carried):
+        first = first_ref[block]
+        packed = in_ref[block, 256:336].astype(f32)[8:]
+        put_queries(packed, first, first_ref[block + 1] - first, columns)
+        return carried
+
+    lax.fori_loop(0, BLOCKS, place, 0, unroll=8)
     total = first_ref[BLOCKS]
     used = (total >> 7) * 128 + 128
 
@@ -248,13 +270,22 @@
 
     lax.fori_loop(0, 4, clear, 0)
     acc[...] = jnp.zeros_like(acc)
-    blocks = (total + 255) >> 9
+
+    largest = unpack_keys(0, in_ref, keys, values)
+    shift, square = start_columns(pl.ds(0, BQ), columns, queries, keys)
+    found = weigh(keys, queries, values, 0, BQ)
+    for chunk in (1, 2):
+        largest = jnp.maximum(largest, unpack_keys(chunk, in_ref, keys, values))
+        found = found + weigh(keys, queries, values, chunk * BK, BQ)
+    acc[:, 0:BQ] = found / found[HD : HD + 1, :]
+    largest_key = jnp.max(largest, axis=1, keepdims=True)
+    blocks = jnp.maximum((total + 255) >> 9, 1)
 
     def block(b, carried):
         attend_columns(b * BQ, BQ, columns, queries, keys, values, acc, largest_key)
         return carried
 
-    lax.fori_loop(0, blocks, block, 0)
+    lax.fori_loop(jnp.where(unsafe(shift, square, largest_key), 0, 1), blocks, block, 0)
 
     @pl.when(total > blocks * BQ)
     def _():
@@ -276,7 +307,7 @@
         out_ref[d] = jnp.concatenate((packed, act_ref[d].astype(f32)), axis=0).astype(bf16)
         return carried
 
-    lax.fori_loop(0, OWNERS, owner, 0)
+    lax.fori_loop(0, OWNERS, owner, 0, unroll=8)
 
 
 def final_kernel(

time: 123 us -> 122 us (level)
  blocking collectives: 29.7 us -> 22.9 us
  Pallas kernels: 46.4 us -> 52.4 us
    all_to_all x1, blocking collectives: 29.7 us -> 22.9 us  [local(): lax.all_to_all(attend_call(first, arrived, pick, act_out), axes, 0, 0, ti...]
    pallas_call x1, Pallas kernels: 34.5 us -> 40.4 us  [attend_call(): pl.pallas_call(attend_kernel, in_specs=[pl.BlockSpec(memory_space=pltpu.S...]
where the time goes in v4:
time: 122 us
  Pallas kernels  52.4 us (43%)
  waiting for transfers between devices  26.5 us (22%)
  blocking collectives  22.9 us (19%)
  starting transfers between devices  9.36 us (8%)
  local copies, waits for them, and re-layouts  4.71 us (4%)
  other arithmetic  4.31 us (4%)
  matrix products  1.57 us (1%)
    pallas_call x1, Pallas kernels, attend_call(): pl.pallas_call(attend_kernel, in_specs=[pl.BlockSpec(memory_space=pltpu.S...  40.4 us
    all_to_all x1, waiting for transfers between devices, local(): arrived = lax.all_to_all(sent, axes, 0, 0, tiled=True)  26.5 us
    all_to_all x1, blocking collectives, local(): lax.all_to_all(attend_call(first, arrived, pick, act_out), axes, 0, 0, ti...  22.9 us
    all_to_all x1, starting transfers between devices, local(): arrived = lax.all_to_all(sent, axes, 0, 0, tiled=True)  9.36 us
    pallas_call x1, Pallas kernels, qkv_call(): pl.pallas_call(qkv_kernel, in_specs=[pl.BlockSpec(memory_space=pltpu.SMEM...  8.68 us
    pallas_call x1, Pallas kernels, finish_call(): pl.pallas_call(final_kernel, in_specs=[vmem()] * 7, out_specs=vmem(), out...  3.23 us
  transfers between devices with their start and end apart: 1, of which 1 were waited for; matrix products, arithmetic and copies ran while one was open for 9% of the time, Pallas kernels for 0%

profile of v4, /device:TPU:0, one launch (start us, length us, event | category | flops | bytes accessed | tf_op | source)
XLA Modules:
  0.0 122.0 jit_solution(7950645410288415896)
XLA Ops:
  0.0 8.7 %projection.1 = bf16[32,336,128]{2,1,0:T(8,128)(2,1)} custom-call(s32[1]{0:T(128)} %bitcast.11.me_ref, bf16[192,1408]{1,0:T(8,128)(2,1)} %bitcast.36, f32[1408]{0:T(1024)} %gain_ref.2, f32[1408]{0:T(1024)} %shift_ref.2, s32[32,192]{1,0:T(8,128)} %lists_ref.1, bf16[1408,4224]{1,0:T(8,128)(2,1)} %w_ref.2, f32[4224]{0:T(1024)} %bias_ref.2), custom_call_target="tpu_custom_call" | custom-call | flops 2283798528 | bytes 14680064 | tf_op jit(solution)/shard_map/projection/pallas_call | solution.py:422
  8.7 9.4 %all-to-all-start = ((bf16[32,336,128]{2,1,0:T(8,128)(2,1)}), bf16[32,336,128]{2,1,0:T(8,128)(2,1)S(1)}, u32[]{:S(2)}, u32[]{:S(2)}) async-start(bf16[32,336,128]{2,1,0:T(8,128)(2,1)} %projection.1), calls=%async_computation | async-start | bytes 5505024 | tf_op jit(solution)/shard_map/all_to_all | solution.py:496
  18.2 0.6 gather_fusion.1
  18.9 0.1 convolution_convert_fusion.1
  19.1 0.6 select_reduce_fusion
  19.7 0.6 convert_reduce_fusion
  20.4 0.7 dynamic_slice.9
  21.4 0.1 fusion.2.first_ref
  21.6 0.1 fusion.1
  22.0 0.1 add_select_fusion
  22.3 0.6 gather_fusion
  23.2 1.2 convolution_convert_fusion
  24.3 1.4 %reshape.230 = bf16[32,6,11,128]{3,2,1,0:T(8,128)(2,1)S(1)} reshape(bf16[192,1408]{1,0:T(8,128)(2,1)} %convolution_convert_fusion) | data formatting | bytes 1081344 | tf_op jit(solution)/shard_map/reshape | solution.py:415
  25.8 0.1 slice.26
  26.0 0.3 fusion.3
  26.3 0.2 copy.30
  26.4 0.7 compare_reduce_fusion
  27.2 0.7 multiply_add_fusion.1
  27.9 0.1 convert_reduce_fusion.1
  28.0 0.7 add_select_fusion.5
  28.9 26.5 %all-to-all-done.in_ref = bf16[32,336,128]{2,1,0:T(8,128)(2,1)S(1)} async-done(((bf16[32,336,128]{2,1,0:T(8,128)(2,1)}), bf16[32,336,128]{2,1,0:T(8,128)(2,1)S(1)}, u32[]{:S(2)}, u32[]{:S(2)}) %all-to-all-start) | async-done | bytes 2752544 | tf_op jit(solution)/shard_map/all_to_all | solution.py:496
  55.4 40.4 %attend.1 = bf16[32,144,128]{2,1,0:T(8,128)(2,1)S(1)} custom-call(s32[40]{0:T(128)S(1)} %fusion.2.first_ref, bf16[32,336,128]{2,1,0:T(8,128)(2,1)S(1)} %all-to-all-done.in_ref, s32[4,768]{1,0:T(4,128)S(1)} %reshape.228.pick_ref, bf16[32,72,128]{2,1,0:T(8,128)(2,1)S(1)} %bitcast.32), custom_call_target="tpu_custom_call" | custom-call | flops 19327352832 | bytes 8388608 | tf_op jit(solution)/shard_map/attend/pallas_call | solution.py:443
  95.9 22.9 %all_to_all.10.in_ref = bf16[32,144,128]{2,1,0:T(8,128)(2,1)S(1)} all-to-all(bf16[32,144,128]{2,1,0:T(8,128)(2,1)S(1)} %attend.1), channel_id=1, replica_groups=mesh['tm'=4,'y'=4,'x'=2,'clip'=4] {'tm','y','x'}, dimensions={0} | all-to-all | bytes 2359296 | tf_op jit(solution)/shard_map/all_to_all | solution.py:501
  118.8 3.2 %finish.1 = bf16[1,192,1408]{2,1,0:T(8,128)(2,1)} custom-call(bf16[32,144,128]{2,1,0:T(8,128)(2,1)S(1)} %all_to_all.10.in_ref, s32[192,128]{1,0:T(8,128)S(1)} %broadcast_in_dim.55.slot_ref, s32[192,128]{1,0:T(8,128)S(1)} %broadcast_in_dim.56.home_ref, bf16[1408,1408]{1,0:T(8,128)(2,1)S(1)} %copy-done, f32[1408]{0:T(1024)S(1)} %copy-done.1, ...), custom_call_target="tpu_custom_call" | custom-call | flops 761266176 | bytes 10485760 | tf_op jit(solution)/shard_map/finish/pallas_call | solution.py:465
  (51 shorter events, 1.6 us)
Async XLA Ops:
  8.7 9.4 %copy-start.7 = (s32[32]{0:T(128)S(1)}, s32[32]{0:T(128)}, u32[]{:S(2)}) copy-start(s32[32]{0:T(128)} %param.21) | copy-start | bytes 388
  8.7 9.4 %copy-start.4 = (s32[32,192]{1,0:T(8,128)S(1)}, s32[32,192]{1,0:T(8,128)}, u32[]{:S(2)}) copy-start(s32[32,192]{1,0:T(8,128)} %lists_ref.1) | copy-start | bytes 73732
  8.7 46.7 %all-to-all-start = ((bf16[32,336,128]{2,1,0:T(8,128)(2,1)}), bf16[32,336,128]{2,1,0:T(8,128)(2,1)S(1)}, u32[]{:S(2)}, u32[]{:S(2)}) async-start(bf16[32,336,128]{2,1,0:T(8,128)(2,1)} %projection.1), calls=%async_computation | async-start | bytes 5505024 | tf_op jit(solution)/shard_map/all_to_all | solution.py:496
  18.1 5.1 %copy-start.5 = (bf16[6,32,1408]{2,1,0:T(8,128)(2,1)S(1)}, bf16[6,32,1408]{2,1,0:T(8,128)(2,1)}, u32[]{:S(2)}) copy-start(bf16[6,32,1408]{2,1,0:T(8,128)(2,1)} %param.11) | copy-start | bytes 1622020
  18.9 0.9 copy-start.6
  55.4 63.4 %copy-start = (bf16[1408,1408]{1,0:T(8,128)(2,1)S(1)}, bf16[1408,1408]{1,0:T(8,128)(2,1)}, u32[]{:S(2)}) copy-start(bf16[1408,1408]{1,0:T(8,128)(2,1)} %w_ref.3) | copy-start | bytes 11894788
  95.9 22.9 %copy-start.1 = (f32[1408]{0:T(1024)S(1)}, f32[1408]{0:T(1024)}, u32[]{:S(2)}) copy-start(f32[1408]{0:T(1024)} %bias_ref.3) | copy-start | bytes 16900
  95.9 22.9 %copy-start.2 = (f32[1408]{0:T(1024)S(1)}, f32[1408]{0:T(1024)}, u32[]{:S(2)}) copy-start(f32[1408]{0:T(1024)} %gain_ref.3) | copy-start | bytes 16900
  95.9 22.9 %copy-start.3 = (f32[1408]{0:T(1024)S(1)}, f32[1408]{0:T(1024)}, u32[]{:S(2)}) copy-start(f32[1408]{0:T(1024)} %shift_ref.3) | copy-start | bytes 16900

commit v5 on v4

--- a/solution.py
+++ b/solution.py
@@ -30,6 +30,7 @@
 SLOTS = 24
 WINDOW = 8 * PART + 128
 BQ = 512
+FIRST = 1024
 BK = 2048
 QK_SCALE = math.log2(math.e) / math.sqrt(HD)
 SAFE = 90.0
@@ -268,28 +269,29 @@
         columns[:, pl.ds(pl.multiple_of(used + i * 128, 128), 128)] = jnp.zeros((HD, 128), f32)
         return carried
 
-    lax.fori_loop(0, 4, clear, 0)
+    lax.fori_loop(0, 9, clear, 0)
     acc[...] = jnp.zeros_like(acc)
 
     largest = unpack_keys(0, in_ref, keys, values)
-    shift, square = start_columns(pl.ds(0, BQ), columns, queries, keys)
-    found = weigh(keys, queries, values, 0, BQ)
+    shift, square = start_columns(pl.ds(0, FIRST), columns, queries, keys)
+    found = weigh(keys, queries, values, 0, FIRST)
     for chunk in (1, 2):
         largest = jnp.maximum(largest, unpack_keys(chunk, in_ref, keys, values))
-        found = found + weigh(keys, queries, values, chunk * BK, BQ)
-    acc[:, 0:BQ] = found / found[HD : HD + 1, :]
+        found = found + weigh(keys, queries, values, chunk * BK, FIRST)
+    acc[:, 0:FIRST] = found / found[HD : HD + 1, :]
     largest_key = jnp.max(largest, axis=1, keepdims=True)
-    blocks = jnp.maximum((total + 255) >> 9, 1)
+    more = jnp.maximum(total - FIRST, 0)
+    blocks = (more + 255) >> 9
 
     def block(b, carried):
-        attend_columns(b * BQ, BQ, columns, queries, keys, values, acc, largest_key)
+        attend_columns(FIRST + b * BQ, BQ, columns, queries, keys, values, acc, largest_key)
         return carried
 
-    lax.fori_loop(jnp.where(unsafe(shift, square, largest_key), 0, 1), blocks, block, 0)
-
-    @pl.when(total > blocks * BQ)
+    lax.fori_loop(jnp.where(unsafe(shift, square, largest_key), -FIRST // BQ, 0), blocks, block, 0)
+
+    @pl.when(more > blocks * BQ)
     def _():
-        attend_columns(blocks * BQ, 256, columns, queries, keys, values, acc, largest_key)
+        attend_columns(FIRST + blocks * BQ, 256, columns, queries, keys, values, acc, largest_key)
 
     for g in range(GROUPS):
         begin = pl.multiple_of((first_ref[8 * g] >> 7) * 128, 128)
@@ -448,12 +450,12 @@
         scratch_shapes=[
             pltpu.VMEM((TOKENS, 256), bf16),
             pltpu.VMEM((HP, TOKENS), bf16),
-            pltpu.VMEM((HD, COLUMNS + 6 * 128), f32),
-            pltpu.VMEM((256, BQ), bf16),
+            pltpu.VMEM((HD, COLUMNS + 10 * 128), f32),
+            pltpu.VMEM((256, FIRST), bf16),
             pltpu.VMEM((HP, COLUMNS + WINDOW), f32),
             pltpu.VMEM((GROUPS, OWNERS * SLOTS, 128), f32),
         ],
-        compiler_params=params(30),
+        compiler_params=params(44),
         cost_estimate=pl.CostEstimate(
             flops=4 * COLUMNS * TOKENS * 256, bytes_accessed=8 * MIB, transcendentals=COLUMNS * TOKENS
         ),
@@ -468,7 +470,7 @@
         out_specs=vmem(),
         out_shape=jax.ShapeDtypeStruct((1, CAP, D), bf16),
         scratch_shapes=[pltpu.VMEM((CAP, HEADS * 128), bf16), pltpu.VMEM((BLOCKS * 8, 9 * 128), f32)],
-        compiler_params=params(30),
+        compiler_params=params(44),
         cost_estimate=pl.CostEstimate(flops=2 * TOK * D * D, bytes_accessed=10 * MIB, transcendentals=0),
         name="finish",
     )(*arrays)

time: 122 us -> 126 us (1.033)
  Pallas kernels: 52.4 us -> 55.4 us
    pallas_call x1, Pallas kernels: 40.4 us -> 43.5 us  [attend_call(): pl.pallas_call(attend_kernel, in_specs=[pl.BlockSpec(memory_space=pltpu.S...]
  transfers between devices with their start and end apart: 1 -> 1, of which waited for: 1 -> 1; matrix products, arithmetic and copies ran while one was open for 9% -> 8% of each run, Pallas kernels for 0% -> 0%
where the time goes in v5:
time: 126 us; the launch traced here: 125 us
  Pallas kernels  55.4 us (44%)
  waiting for transfers between devices  26.3 us (21%)
  blocking collectives  23.2 us (18%)
  starting transfers between devices  9.54 us (8%)
  local copies, waits for them, and re-layouts  4.71 us (4%)
  other arithmetic  4.31 us (3%)
  matrix products  1.57 us (1%)
    pallas_call x1, Pallas kernels, attend_call(): pl.pallas_call(attend_kernel, in_specs=[pl.BlockSpec(memory_space=pltpu.S...  43.5 us
    all_to_all x1, waiting for transfers between devices, local(): arrived = lax.all_to_all(sent, axes, 0, 0, tiled=True)  26.3 us
    all_to_all x1, blocking collectives, local(): lax.all_to_all(attend_call(first, arrived, pick, act_out), axes, 0, 0, ti...  23.2 us
    all_to_all x1, starting transfers between devices, local(): arrived = lax.all_to_all(sent, axes, 0, 0, tiled=True)  9.54 us
    pallas_call x1, Pallas kernels, qkv_call(): pl.pallas_call(qkv_kernel, in_specs=[pl.BlockSpec(memory_space=pltpu.SMEM...  8.68 us
    pallas_call x1, Pallas kernels, finish_call(): pl.pallas_call(final_kernel, in_specs=[vmem()] * 7, out_specs=vmem(), out...  3.23 us
  transfers between devices with their start and end apart: 1, of which 1 were waited for; matrix products, arithmetic and copies ran while one was open for 8% of the time, Pallas kernels for 0%

profile of v5, /device:TPU:0, one launch (start us, length us, event | category | flops | bytes accessed | tf_op | source)
XLA Modules:
  0.0 125.4 jit_solution(14955258656867992939)
XLA Ops:
  0.0 8.7 %projection.1 = bf16[32,336,128]{2,1,0:T(8,128)(2,1)} custom-call(s32[1]{0:T(128)} %bitcast.11.me_ref, bf16[192,1408]{1,0:T(8,128)(2,1)} %bitcast.36, f32[1408]{0:T(1024)} %gain_ref.2, f32[1408]{0:T(1024)} %shift_ref.2, s32[32,192]{1,0:T(8,128)} %lists_ref.1, bf16[1408,4224]{1,0:T(8,128)(2,1)} %w_ref.2, f32[4224]{0:T(1024)} %bias_ref.2), custom_call_target="tpu_custom_call" | custom-call | flops 2283798528 | bytes 14680064 | tf_op jit(solution)/shard_map/projection/pallas_call | solution.py:424
  8.7 9.5 %all-to-all-start = ((bf16[32,336,128]{2,1,0:T(8,128)(2,1)}), bf16[32,336,128]{2,1,0:T(8,128)(2,1)S(1)}, u32[]{:S(2)}, u32[]{:S(2)}) async-start(bf16[32,336,128]{2,1,0:T(8,128)(2,1)} %projection.1), calls=%async_computation | async-start | bytes 5505024 | tf_op jit(solution)/shard_map/all_to_all | solution.py:498
  18.3 0.6 gather_fusion.1
  19.1 0.1 convolution_convert_fusion.1
  19.3 0.6 select_reduce_fusion
  19.9 0.6 convert_reduce_fusion
  20.5 0.7 dynamic_slice.9
  21.6 0.1 fusion.2.first_ref
  21.8 0.1 fusion.1
  22.2 0.1 add_select_fusion
  22.4 0.6 gather_fusion
  23.4 1.2 convolution_convert_fusion
  24.5 1.4 %reshape.230 = bf16[32,6,11,128]{3,2,1,0:T(8,128)(2,1)S(1)} reshape(bf16[192,1408]{1,0:T(8,128)(2,1)} %convolution_convert_fusion) | data formatting | bytes 1081344 | tf_op jit(solution)/shard_map/reshape | solution.py:417
  25.9 0.1 slice.26
  26.2 0.3 fusion.3
  26.4 0.2 copy.30
  26.6 0.7 compare_reduce_fusion
  27.4 0.7 multiply_add_fusion.1
  28.1 0.1 convert_reduce_fusion.1
  28.2 0.7 add_select_fusion.5
  29.1 26.3 %all-to-all-done.in_ref = bf16[32,336,128]{2,1,0:T(8,128)(2,1)S(1)} async-done(((bf16[32,336,128]{2,1,0:T(8,128)(2,1)}), bf16[32,336,128]{2,1,0:T(8,128)(2,1)S(1)}, u32[]{:S(2)}, u32[]{:S(2)}) %all-to-all-start) | async-done | bytes 2752544 | tf_op jit(solution)/shard_map/all_to_all | solution.py:498
  55.4 43.5 %attend.1 = bf16[32,144,128]{2,1,0:T(8,128)(2,1)S(1)} custom-call(s32[40]{0:T(128)S(1)} %fusion.2.first_ref, bf16[32,336,128]{2,1,0:T(8,128)(2,1)S(1)} %all-to-all-done.in_ref, s32[4,768]{1,0:T(4,128)S(1)} %reshape.228.pick_ref, bf16[32,72,128]{2,1,0:T(8,128)(2,1)S(1)} %bitcast.32), custom_call_target="tpu_custom_call" | custom-call | flops 19327352832 | bytes 8388608 | tf_op jit(solution)/shard_map/attend/pallas_call | solution.py:445
  99.0 23.2 %all_to_all.10.in_ref = bf16[32,144,128]{2,1,0:T(8,128)(2,1)S(1)} all-to-all(bf16[32,144,128]{2,1,0:T(8,128)(2,1)S(1)} %attend.1), channel_id=1, replica_groups=mesh['tm'=4,'y'=4,'x'=2,'clip'=4] {'tm','y','x'}, dimensions={0} | all-to-all | bytes 2359296 | tf_op jit(solution)/shard_map/all_to_all | solution.py:503
  122.2 3.2 %finish.1 = bf16[1,192,1408]{2,1,0:T(8,128)(2,1)} custom-call(bf16[32,144,128]{2,1,0:T(8,128)(2,1)S(1)} %all_to_all.10.in_ref, s32[192,128]{1,0:T(8,128)S(1)} %broadcast_in_dim.55.slot_ref, s32[192,128]{1,0:T(8,128)S(1)} %broadcast_in_dim.56.home_ref, bf16[1408,1408]{1,0:T(8,128)(2,1)S(1)} %copy-done, f32[1408]{0:T(1024)S(1)} %copy-done.1, ...), custom_call_target="tpu_custom_call" | custom-call | flops 761266176 | bytes 10485760 | tf_op jit(solution)/shard_map/finish/pallas_call | solution.py:467
  (51 shorter events, 1.6 us)
Async XLA Ops:
  8.7 9.6 %copy-start.7 = (s32[32]{0:T(128)S(1)}, s32[32]{0:T(128)}, u32[]{:S(2)}) copy-start(s32[32]{0:T(128)} %param.21) | copy-start | bytes 388
  8.7 9.6 %copy-start.4 = (s32[32,192]{1,0:T(8,128)S(1)}, s32[32,192]{1,0:T(8,128)}, u32[]{:S(2)}) copy-start(s32[32,192]{1,0:T(8,128)} %lists_ref.1) | copy-start | bytes 73732
  8.7 46.7 %all-to-all-start = ((bf16[32,336,128]{2,1,0:T(8,128)(2,1)}), bf16[32,336,128]{2,1,0:T(8,128)(2,1)S(1)}, u32[]{:S(2)}, u32[]{:S(2)}) async-start(bf16[32,336,128]{2,1,0:T(8,128)(2,1)} %projection.1), calls=%async_computation | async-start | bytes 5505024 | tf_op jit(solution)/shard_map/all_to_all | solution.py:498
  18.3 5.1 %copy-start.5 = (bf16[6,32,1408]{2,1,0:T(8,128)(2,1)S(1)}, bf16[6,32,1408]{2,1,0:T(8,128)(2,1)}, u32[]{:S(2)}) copy-start(bf16[6,32,1408]{2,1,0:T(8,128)(2,1)} %param.11) | copy-start | bytes 1622020
  19.1 0.9 copy-start.6
  55.4 66.7 %copy-start = (bf16[1408,1408]{1,0:T(8,128)(2,1)S(1)}, bf16[1408,1408]{1,0:T(8,128)(2,1)}, u32[]{:S(2)}) copy-start(bf16[1408,1408]{1,0:T(8,128)(2,1)} %w_ref.3) | copy-start | bytes 11894788
  98.9 23.2 %copy-start.1 = (f32[1408]{0:T(1024)S(1)}, f32[1408]{0:T(1024)}, u32[]{:S(2)}) copy-start(f32[1408]{0:T(1024)} %bias_ref.3) | copy-start | bytes 16900
  98.9 23.2 %copy-start.2 = (f32[1408]{0:T(1024)S(1)}, f32[1408]{0:T(1024)}, u32[]{:S(2)}) copy-start(f32[1408]{0:T(1024)} %gain_ref.3) | copy-start | bytes 16900
  99.0 23.2 %copy-start.3 = (f32[1408]{0:T(1024)S(1)}, f32[1408]{0:T(1024)}, u32[]{:S(2)}) copy-start(f32[1408]{0:T(1024)} %shift_ref.3) | copy-start | bytes 16900

commit v6 on v4

--- a/solution.py
+++ b/solution.py
@@ -58,11 +58,15 @@
     return lax.broadcasted_iota(jnp.int32, shape, 1) < bound
 
 
+def block_number(z, y, x):
+    return x * 16 + y * 4 + z
+
+
 def where_tokens(lists):
     token = jnp.maximum(lists, 0)
     frame, patch = token >> 8, token & 255
     z = (frame * 43) >> 8
-    return z * 8 + (patch >> 5), (frame - z * 6) * 32 + (patch & 31)
+    return block_number(z, patch >> 6, (patch >> 5) & 1), (frame - z * 6) * 32 + (patch & 31)
 
 
 def ones_where(condition):
@@ -139,7 +143,7 @@
                 (asked[x, h * HD + QROWS : h * HD + HD, :], jnp.zeros((8, 128), f32)), axis=0
             )
             spread = jnp.concatenate((last, pltpu.roll(last, 64, 1), pltpu.roll(last, 32, 1)), axis=0)
-            out_ref[2 * h + x] = jnp.concatenate(
+            out_ref[block_number(h // 4, h % 4, x)] = jnp.concatenate(
                 (main[k_rows, :], main[v_rows, :], both, jnp.where(queries, top, spread)), axis=0
             ).astype(bf16)
 
@@ -365,7 +369,7 @@
     return jnp.dot(earlier, values.astype(bf16), preferred_element_type=f32).astype(jnp.int32)
 
 
-def routes(mask_tokens, assignment, me_x, me_block):
+def routes(mask_tokens, assignment, me_x, me_block, me_owner):
     blocks, _ = where_tokens(mask_tokens)
     listed = mask_tokens >= 0
     hit = listed[:, :, None] & (blocks[:, :, None] == jnp.arange(BLOCKS)[None, None, :])
@@ -392,13 +396,14 @@
     hit = here[:, :, None] & (order[:, :, None] == jnp.arange(8)[None, None, :])
     act_pick = jnp.sum(jnp.where(hit, local[:, :, None] + 1, 0), axis=1) - 1
 
-    own = lax.dynamic_index_in_dim(lists, me_block, 0, keepdims=False)
+    own = lax.dynamic_index_in_dim(lists, me_owner, 0, keepdims=False)
     own_block, _ = where_tokens(own)
     same = (own_block[:, None] == own_block[None, :]) & (own >= 0)[:, None]
     order = jnp.sum((same & (entry[:, None] < entry[None, :])).astype(jnp.int32), axis=0)
-    half = (order + own_block + lax.dynamic_index_in_dim(assignment, me_block, 0, keepdims=False)) % 2
+    half = (order + own_block + lax.dynamic_index_in_dim(assignment, me_owner, 0, keepdims=False)) % 2
     slot = jnp.where(own >= 0, half * PART + own_block * 3 + order // 2, -1)
-    home = jnp.where(own >= 0, own_block * 8 + order, -1)
+    sender = (own_block & 3) * 8 + ((own_block >> 2) & 3) * 2 + (own_block >> 4)
+    home = jnp.where(own >= 0, sender * 8 + order, -1)
     wide = (CAP, 128)
     return (
         first,
@@ -490,12 +495,13 @@
     tokens = activations.reshape(TOK, D)
     axes = ("tm", "y", "x")
     me_x = lax.axis_index("x")
-    me_block = lax.axis_index("tm") * 8 + lax.axis_index("y") * 2 + me_x
+    me_block = block_number(lax.axis_index("tm"), lax.axis_index("y"), me_x)
+    me_owner = lax.axis_index("tm") * 8 + lax.axis_index("y") * 2 + me_x
 
     sent = qkv_call(me_block[None], tokens, attn_gain, attn_shift, mask_tokens, w_qkv, b_qkv)
-    arrived = lax.all_to_all(sent, axes, 0, 0, tiled=True)
-
-    first, pick, act_pick, slot, home = routes(mask_tokens, assignment, me_x, me_block)
+    arrived = lax.all_to_all(sent, ("x", "y", "tm"), 0, 0, tiled=True)
+
+    first, pick, act_pick, slot, home = routes(mask_tokens, assignment, me_x, me_block, me_owner)
     act_out = pack_rows(act_pick, tokens)
     first, pick, act_out, slot, home = lax.optimization_barrier((first, pick, act_out, slot, home))
     o_in = lax.all_to_all(attend_call(first, arrived, pick, act_out), axes, 0, 0, tiled=True)

time: 122 us -> 124 us (1.016)
  blocking collectives: 22.9 us -> 25 us
    all_to_all x1, blocking collectives: 22.9 us -> 25 us  [local(): lax.all_to_all(attend_call(first, arrived, pick, act_out), axes, 0, 0, ti...]
where the time goes in v6:
time: 124 us
  Pallas kernels  52.4 us (42%)
  waiting for transfers between devices  25.8 us (21%)
  blocking collectives  25 us (20%)
  starting transfers between devices  9.36 us (8%)
  local copies, waits for them, and re-layouts  4.71 us (4%)
  other arithmetic  4.32 us (3%)
  matrix products  1.57 us (1%)
    pallas_call x1, Pallas kernels, attend_call(): pl.pallas_call(attend_kernel, in_specs=[pl.BlockSpec(memory_space=pltpu.S...  40.5 us
    all_to_all x1, waiting for transfers between devices, local(): arrived = lax.all_to_all(sent, ('x', 'y', 'tm'), 0, 0, tiled=True)  25.8 us
    all_to_all x1, blocking collectives, local(): lax.all_to_all(attend_call(first, arrived, pick, act_out), axes, 0, 0, ti...  25 us
    all_to_all x1, starting transfers between devices, local(): arrived = lax.all_to_all(sent, ('x', 'y', 'tm'), 0, 0, tiled=True)  9.36 us
    pallas_call x1, Pallas kernels, qkv_call(): pl.pallas_call(qkv_kernel, in_specs=[pl.BlockSpec(memory_space=pltpu.SMEM...  8.68 us
    pallas_call x1, Pallas kernels, finish_call(): pl.pallas_call(final_kernel, in_specs=[vmem()] * 7, out_specs=vmem(), out...  3.23 us
  transfers between devices with their start and end apart: 1, of which 1 were waited for; matrix products, arithmetic and copies ran while one was open for 9% of the time, Pallas kernels for 0%

profile of v6, /device:TPU:0, one launch (start us, length us, event | category | flops | bytes accessed | tf_op | source)
XLA Modules:
  0.0 123.6 jit_solution(11546698722012436534)
XLA Ops:
  0.0 8.7 %projection.1 = bf16[32,336,128]{2,1,0:T(8,128)(2,1)} custom-call(s32[1]{0:T(128)} %bitcast.11.me_ref, bf16[192,1408]{1,0:T(8,128)(2,1)} %bitcast.36, f32[1408]{0:T(1024)} %gain_ref.2, f32[1408]{0:T(1024)} %shift_ref.2, s32[32,192]{1,0:T(8,128)} %lists_ref.1, bf16[1408,4224]{1,0:T(8,128)(2,1)} %w_ref.2, f32[4224]{0:T(1024)} %bias_ref.2), custom_call_target="tpu_custom_call" | custom-call | flops 2283798528 | bytes 14680064 | tf_op jit(solution)/shard_map/projection/pallas_call | solution.py:427
  8.7 9.4 %all-to-all-start = ((bf16[32,336,128]{2,1,0:T(8,128)(2,1)}), bf16[32,336,128]{2,1,0:T(8,128)(2,1)S(1)}, u32[]{:S(2)}, u32[]{:S(2)}) async-start(bf16[32,336,128]{2,1,0:T(8,128)(2,1)} %projection.1), calls=%async_computation | async-start | bytes 5505024 | tf_op jit(solution)/shard_map/all_to_all | solution.py:502
  18.2 0.6 gather_fusion.1
  18.9 0.1 convolution_convert_fusion.1
  19.1 0.6 select_reduce_fusion
  19.7 0.6 convert_reduce_fusion
  20.4 0.7 dynamic_slice.9
  21.4 0.1 fusion.2.first_ref
  21.6 0.1 fusion.1
  22.0 0.1 add_select_fusion
  22.3 0.6 gather_fusion
  23.2 1.2 convolution_convert_fusion
  24.4 1.4 %reshape.252 = bf16[32,6,11,128]{3,2,1,0:T(8,128)(2,1)S(1)} reshape(bf16[192,1408]{1,0:T(8,128)(2,1)} %convolution_convert_fusion) | data formatting | bytes 1081344 | tf_op jit(solution)/shard_map/reshape | solution.py:420
  25.8 0.1 slice.26
  26.0 0.3 fusion.3
  26.3 0.2 copy.30
  26.5 0.7 compare_reduce_fusion
  27.2 0.7 add_add_fusion.1
  27.9 0.1 convert_reduce_fusion.1
  28.0 0.7 add_select_fusion.5
  28.9 25.8 %all-to-all-done.in_ref = bf16[32,336,128]{2,1,0:T(8,128)(2,1)S(1)} async-done(((bf16[32,336,128]{2,1,0:T(8,128)(2,1)}), bf16[32,336,128]{2,1,0:T(8,128)(2,1)S(1)}, u32[]{:S(2)}, u32[]{:S(2)}) %all-to-all-start) | async-done | bytes 2752544 | tf_op jit(solution)/shard_map/all_to_all | solution.py:502
  54.8 40.5 %attend.1 = bf16[32,144,128]{2,1,0:T(8,128)(2,1)S(1)} custom-call(s32[40]{0:T(128)S(1)} %fusion.2.first_ref, bf16[32,336,128]{2,1,0:T(8,128)(2,1)S(1)} %all-to-all-done.in_ref, s32[4,768]{1,0:T(4,128)S(1)} %reshape.250.pick_ref, bf16[32,72,128]{2,1,0:T(8,128)(2,1)S(1)} %bitcast.32), custom_call_target="tpu_custom_call" | custom-call | flops 19327352832 | bytes 8388608 | tf_op jit(solution)/shard_map/attend/pallas_call | solution.py:448
  95.3 25.0 %all_to_all.10.in_ref = bf16[32,144,128]{2,1,0:T(8,128)(2,1)S(1)} all-to-all(bf16[32,144,128]{2,1,0:T(8,128)(2,1)S(1)} %attend.1), channel_id=1, replica_groups=mesh['tm'=4,'y'=4,'x'=2,'clip'=4] {'tm','y','x'}, dimensions={0} | all-to-all | bytes 2359296 | tf_op jit(solution)/shard_map/all_to_all | solution.py:507
  120.3 3.2 %finish.1 = bf16[1,192,1408]{2,1,0:T(8,128)(2,1)} custom-call(bf16[32,144,128]{2,1,0:T(8,128)(2,1)S(1)} %all_to_all.10.in_ref, s32[192,128]{1,0:T(8,128)S(1)} %broadcast_in_dim.55.slot_ref, s32[192,128]{1,0:T(8,128)S(1)} %broadcast_in_dim.56.home_ref, bf16[1408,1408]{1,0:T(8,128)(2,1)S(1)} %copy-done, f32[1408]{0:T(1024)S(1)} %copy-done.1, ...), custom_call_target="tpu_custom_call" | custom-call | flops 761266176 | bytes 10485760 | tf_op jit(solution)/shard_map/finish/pallas_call | solution.py:470
  (51 shorter events, 1.6 us)
Async XLA Ops:
  8.7 9.4 %copy-start.7 = (s32[32]{0:T(128)S(1)}, s32[32]{0:T(128)}, u32[]{:S(2)}) copy-start(s32[32]{0:T(128)} %param.21) | copy-start | bytes 388
  8.7 9.4 %copy-start.4 = (s32[32,192]{1,0:T(8,128)S(1)}, s32[32,192]{1,0:T(8,128)}, u32[]{:S(2)}) copy-start(s32[32,192]{1,0:T(8,128)} %lists_ref.1) | copy-start | bytes 73732
  8.7 46.1 %all-to-all-start = ((bf16[32,336,128]{2,1,0:T(8,128)(2,1)}), bf16[32,336,128]{2,1,0:T(8,128)(2,1)S(1)}, u32[]{:S(2)}, u32[]{:S(2)}) async-start(bf16[32,336,128]{2,1,0:T(8,128)(2,1)} %projection.1), calls=%async_computation | async-start | bytes 5505024 | tf_op jit(solution)/shard_map/all_to_all | solution.py:502
  18.1 5.1 %copy-start.5 = (bf16[6,32,1408]{2,1,0:T(8,128)(2,1)S(1)}, bf16[6,32,1408]{2,1,0:T(8,128)(2,1)}, u32[]{:S(2)}) copy-start(bf16[6,32,1408]{2,1,0:T(8,128)(2,1)} %param.11) | copy-start | bytes 1622020
  18.9 0.9 copy-start.6
  54.8 65.5 %copy-start = (bf16[1408,1408]{1,0:T(8,128)(2,1)S(1)}, bf16[1408,1408]{1,0:T(8,128)(2,1)}, u32[]{:S(2)}) copy-start(bf16[1408,1408]{1,0:T(8,128)(2,1)} %w_ref.3) | copy-start | bytes 11894788
  95.2 25.1 %copy-start.1 = (f32[1408]{0:T(1024)S(1)}, f32[1408]{0:T(1024)}, u32[]{:S(2)}) copy-start(f32[1408]{0:T(1024)} %bias_ref.3) | copy-start | bytes 16900
  95.3 25.1 %copy-start.2 = (f32[1408]{0:T(1024)S(1)}, f32[1408]{0:T(1024)}, u32[]{:S(2)}) copy-start(f32[1408]{0:T(1024)} %gain_ref.3) | copy-start | bytes 16900
  95.3 25.1 %copy-start.3 = (f32[1408]{0:T(1024)S(1)}, f32[1408]{0:T(1024)}, u32[]{:S(2)}) copy-start(f32[1408]{0:T(1024)} %shift_ref.3) | copy-start | bytes 16900
